TPU v7x, 128 devices: a whole 4x4x4 slice. The times are simulated.
128 devices in a mesh: dp: 32 (over x, z, core), row: 2 (over y_lo), col: 2 (over y_hi).
Axes of the slice: x: 4, y: 4 (y_hi: 2, y_lo: 2; y = y_hi * 2 + y_lo), z: 4, core: 2. Of those that a mesh axis runs over, the one named last changes fastest.
Arguments:
- activations: bfloat16 [16384, 768], P(('dp', 'row'), 'col'), may hold values from -6 to 6
- timesteps: int32 [64], P(('dp', 'col')), may hold values from 0 to 999
- class_labels: int32 [64], P(('dp', 'col')), may hold values from 0 to 1000
- time_table: bfloat16 [1000, 768], P(None, 'row'), may hold values from -4 to 4
- class_table: bfloat16 [1001, 768], P(None, 'row'), may hold values from -4 to 4
- modulation: bfloat16 [768, 6, 768], P('row', None, 'col'), may hold values from -0.21875 to 0.21875
- modulation_bias: bfloat16 [6, 768], P(None, 'col'), may hold values from -3 to 3
- attention: bfloat16 [768, 3, 768], P('col', None, 'row'), may hold values from -0.21875 to 0.21875
- attention_bias: bfloat16 [2, 768], P(None, 'row'), may hold values from -2 to 2
- projection: bfloat16 [768, 768], P('row', 'col'), may hold values from -0.875 to 0.875
- projection_bias: bfloat16 [768], P('col'), may hold values from -2 to 2
- expansion: bfloat16 [768, 3072], P('col', 'row'), may hold values from -0.21875 to 0.21875
- widening_bias: bfloat16 [3072], P('row'), may hold values from -2 to 2
- reduction: bfloat16 [3072, 768], P('row', 'col'), may hold values from -0.109375 to 0.109375
- narrowing_bias: bfloat16 [768], P('col'), may hold values from -2 to 2
- cotangent: bfloat16 [16384, 768], P(('dp', 'row'), 'col'), may hold values from -6 to 6
Outputs:
- result: bfloat16 [16384, 768], P(('dp', 'row'), 'col')
- activations_grad: float32 [16384, 768], P(('dp', 'row'), 'col')
- time_grad: float32 [1000, 768], P(None, 'row')
- class_grad: float32 [1001, 768], P(None, 'row')
- modulation_grad: float32 [768, 6, 768], P('row', None, 'col')
- modulation_bias_grad: float32 [6, 768], P(None, 'col')
- attention_grad: float32 [768, 3, 768], P('col', None, 'row')
- attention_bias_grad: float32 [2, 768], P(None, 'row')
- projection_grad: float32 [768, 768], P('row', 'col')
- projection_bias_grad: float32 [768], P('col')
- expansion_grad: float32 [768, 3072], P('col', 'row')
- expansion_bias_grad: float32 [3072], P('row')
- reduction_grad: float32 [3072, 768], P('row', 'col')
- reduction_bias_grad: float32 [768], P('col')
Inputs may be any that keep to these rules, and one draw needn't show every extreme that they name: `timesteps`: row of time_table used by each latent. `class_labels`: row of class_table used by each latent.
All inputs are finite; a program needn't handle non-finite values.
Results may differ from a plain program's by a relative error of at most 0.02.
Values may be sent and summed in bfloat16 or wider, within the bound.
A program may use at most 128 MiB of HBM per device.

v0:
```python
import jax
import jax.numpy as jnp
from jax import lax
from jax.sharding import PartitionSpec as P

D = 768
HEAD_DIM = 64
STEPS = 1000
CLASSES = 1001
SEQ = 256


EPSILON = 1e-06


def product_rows(row_piece, matrix, transposed):
    if transposed:
        return lax.dot_general(
            row_piece, matrix, (((1,), (1,)), ((), ())), preferred_element_type=jnp.float32
        )
    return jnp.dot(row_piece, matrix, preferred_element_type=jnp.float32)


def through_rows(local_rows, matrix, transposed):
    gathered = lax.all_gather(local_rows, "row", axis=0, tiled=True)
    keep_rows = gathered.shape[0] // lax.axis_size("col")

    def row_term(first_row, row_count):
        return product_rows(gathered, matrix, transposed)

    summed = lax.psum_scatter(
        row_term(jnp.int32(0), keep_rows * lax.axis_size("col")),
        "col",
        scatter_dimension=0,
        tiled=True,
    )
    return (summed, gathered)


def through_cols(local_rows, matrix, transposed):
    gathered = lax.all_gather(local_rows, "col", axis=0, tiled=True)
    keep_rows = gathered.shape[0] // lax.axis_size("row")

    def row_term(first_row, row_count):
        return product_rows(gathered, matrix, transposed)

    summed = lax.psum_scatter(
        row_term(jnp.int32(0), keep_rows * lax.axis_size("row")),
        "row",
        scatter_dimension=0,
        tiled=True,
    )
    return (summed, gathered)


def column_totals(first_terms, second_terms):
    return lax.psum((jnp.sum(first_terms, axis=-1), jnp.sum(second_terms, axis=-1)), "col")


def normalize(values, full_width):
    row_total, squares = column_totals(values, values * values)
    average = row_total / full_width
    inverse = lax.rsqrt(squares / full_width - average * average + EPSILON)
    return ((values - average[..., None]) * inverse[..., None], inverse)


def normalize_back(grad_normed, normed, inverse, full_width):
    row_total, crossed = column_totals(grad_normed, grad_normed * normed)
    centered = (
        grad_normed
        - (row_total / full_width)[..., None]
        - normed * (crossed / full_width)[..., None]
    )
    return inverse[..., None] * centered


def weight_gradient(gathered_in, gathered_grad):
    return lax.dot_general(
        gathered_in, gathered_grad, (((0,), (0,)), ((), ())), preferred_element_type=jnp.float32
    )


def settle(weight_grad, bias_grad):
    return (weight_grad, bias_grad)


def gelu_tanh(values):
    return jax.nn.gelu(values, approximate=True)


def table_product(onehot_rows, grad_rows):
    return lax.dot_general(
        onehot_rows, grad_rows, (((0,), (0,)), ((), ())), precision=lax.Precision.HIGHEST
    )


def body(
    activations,
    timesteps,
    class_labels,
    time_table,
    class_table,
    modulation,
    modulation_bias,
    attention,
    attention_bias,
    projection,
    projection_bias,
    expansion,
    widening_bias,
    reduction,
    narrowing_bias,
    cotangent,
):
    half_cols = activations.shape[1]
    half_rows = time_table.shape[1]
    tokens_a = activations.shape[0]
    latents_a = tokens_a // SEQ
    latents_b = timesteps.shape[0]
    tokens_b = latents_b * SEQ
    head_count = half_rows // HEAD_DIM
    score_scale = HEAD_DIM ** (-0.5)
    time_onehot = (timesteps[:, None] == jnp.arange(STEPS, dtype=jnp.int32)[None, :]).astype(
        jnp.bfloat16
    )
    class_onehot = (class_labels[:, None] == jnp.arange(CLASSES, dtype=jnp.int32)[None, :]).astype(
        jnp.bfloat16
    )
    condition = jnp.dot(time_onehot, time_table, preferred_element_type=jnp.float32) + jnp.dot(
        class_onehot, class_table, preferred_element_type=jnp.float32
    )
    silu_cond, silu_pullback = jax.vjp(jax.nn.silu, condition)
    silu_low = silu_cond.astype(jnp.bfloat16)
    modulation_flat = modulation.reshape(half_rows, 6 * half_cols)
    modulated_sum, cond_gathered = through_cols(silu_low, modulation_flat, False)
    modulation_values = modulated_sum.reshape(latents_a, 6, half_cols) + modulation_bias
    shift_first = modulation_values[:, 0][:, None, :]
    scale_first = modulation_values[:, 1][:, None, :]
    gate_first = modulation_values[:, 2][:, None, :]
    shift_second = modulation_values[:, 3][:, None, :]
    scale_second = modulation_values[:, 4][:, None, :]
    gate_second = modulation_values[:, 5][:, None, :]
    residual = activations.astype(jnp.float32).reshape(latents_a, SEQ, half_cols)
    normed_first, inverse_first = normalize(residual, D)
    hidden_first = (
        (normed_first * (1.0 + scale_first) + shift_first)
        .astype(jnp.bfloat16)
        .reshape(tokens_a, half_cols)
    )
    attention_flat = attention.reshape(half_cols, 3 * half_rows)
    triple_sum, hidden_first_all = through_rows(hidden_first, attention_flat, False)
    zero_bias = jnp.zeros_like(attention_bias[0])
    triple_bias = jnp.stack([attention_bias[0], zero_bias, attention_bias[1]])
    triple = triple_sum.reshape(tokens_b, 3, half_rows) + triple_bias
    query_heads = triple[:, 0].astype(jnp.bfloat16).reshape(latents_b, SEQ, head_count, HEAD_DIM)
    key_heads = triple[:, 1].astype(jnp.bfloat16).reshape(latents_b, SEQ, head_count, HEAD_DIM)
    value_heads = triple[:, 2].astype(jnp.bfloat16).reshape(latents_b, SEQ, head_count, HEAD_DIM)
    scores = (
        jnp.einsum("lqhd,lkhd->lhqk", query_heads, key_heads, preferred_element_type=jnp.float32)
        * score_scale
    )
    highest = jnp.max(scores, axis=-1, keepdims=True)
    exponent = jnp.exp(scores - highest)
    totals = jnp.sum(exponent, axis=-1, keepdims=True)
    softmax_weights = exponent / totals
    log_total = highest + jnp.log(totals)
    mixture = jnp.einsum(
        "lhqk,lkhd->lqhd",
        softmax_weights.astype(jnp.bfloat16),
        value_heads,
        preferred_element_type=jnp.float32,
    )
    attended = mixture.astype(jnp.bfloat16).reshape(tokens_b, half_rows)
    projected, attended_all = through_cols(attended, projection, False)
    branch_first = (projected + projection_bias).reshape(latents_a, SEQ, half_cols)
    residual_mid = residual + gate_first * branch_first
    normed_second, inverse_second = normalize(residual_mid, D)
    hidden_after_feedforward = (
        (normed_second * (1.0 + scale_second) + shift_second)
        .astype(jnp.bfloat16)
        .reshape(tokens_a, half_cols)
    )
    expanded_sum, hidden_second_all = through_rows(hidden_after_feedforward, expansion, False)
    expanded_hidden_rows = expanded_sum + widening_bias
    gelu_activated_rows, gelu_pullback = jax.vjp(gelu_tanh, expanded_hidden_rows)
    activated_low = gelu_activated_rows.astype(jnp.bfloat16)
    reduced, activated_all = through_cols(activated_low, reduction, False)
    feedforward_branch_output = (reduced + narrowing_bias).reshape(latents_a, SEQ, half_cols)
    finished = residual_mid + gate_second * feedforward_branch_output
    result = finished.astype(jnp.bfloat16).reshape(tokens_a, half_cols)
    grad_finished = cotangent.astype(jnp.float32).reshape(latents_a, SEQ, half_cols)
    grad_gate_second = jnp.sum(grad_finished * feedforward_branch_output, axis=1)
    grad_branch_second = (
        (grad_finished * gate_second).astype(jnp.bfloat16).reshape(tokens_a, half_cols)
    )
    grad_activated, grad_second_all = through_rows(grad_branch_second, reduction, True)
    reduction_grad, reduction_bias_grad = settle(
        weight_gradient(activated_all, grad_second_all),
        jnp.sum(grad_second_all, axis=0, dtype=jnp.float32),
    )
    grad_expanded = gelu_pullback(grad_activated)[0].astype(jnp.bfloat16)
    grad_hidden_second_sum, grad_expanded_all = through_cols(grad_expanded, expansion, True)
    expansion_grad, expansion_bias_grad = settle(
        weight_gradient(hidden_second_all, grad_expanded_all),
        jnp.sum(grad_expanded_all, axis=0, dtype=jnp.float32),
    )
    grad_hidden_second = grad_hidden_second_sum.reshape(latents_a, SEQ, half_cols)
    grad_shift_second = jnp.sum(grad_hidden_second, axis=1)
    grad_scale_second = jnp.sum(grad_hidden_second * normed_second, axis=1)
    grad_residual_mid = grad_finished + normalize_back(
        grad_hidden_second * (1.0 + scale_second), normed_second, inverse_second, D
    )
    grad_gate_first = jnp.sum(grad_residual_mid * branch_first, axis=1)
    grad_branch_first = (
        (grad_residual_mid * gate_first).astype(jnp.bfloat16).reshape(tokens_a, half_cols)
    )
    grad_attended_sum, grad_first_all = through_rows(grad_branch_first, projection, True)
    projection_grad, projection_bias_grad = settle(
        weight_gradient(attended_all, grad_first_all),
        jnp.sum(grad_first_all, axis=0, dtype=jnp.float32),
    )
    grad_mixture = grad_attended_sum.astype(jnp.bfloat16).reshape(
        latents_b, SEQ, head_count, HEAD_DIM
    )
    scores_again = (
        jnp.einsum("lqhd,lkhd->lhqk", query_heads, key_heads, preferred_element_type=jnp.float32)
        * score_scale
    )
    weights_again = jnp.exp(scores_again - log_total)
    grad_weights = jnp.einsum(
        "lqhd,lkhd->lhqk", grad_mixture, value_heads, preferred_element_type=jnp.float32
    )
    grad_values = jnp.einsum(
        "lhqk,lqhd->lkhd",
        weights_again.astype(jnp.bfloat16),
        grad_mixture,
        preferred_element_type=jnp.float32,
    )
    centered = jnp.sum(grad_weights * weights_again, axis=-1, keepdims=True)
    grad_scores = (weights_again * (grad_weights - centered)).astype(jnp.bfloat16)
    grad_query = (
        jnp.einsum("lhqk,lkhd->lqhd", grad_scores, key_heads, preferred_element_type=jnp.float32)
        * score_scale
    )
    grad_keys = (
        jnp.einsum("lhqk,lqhd->lkhd", grad_scores, query_heads, preferred_element_type=jnp.float32)
        * score_scale
    )
    grad_triple = jnp.stack(
        [
            grad_query.reshape(tokens_b, half_rows),
            grad_keys.reshape(tokens_b, half_rows),
            grad_values.reshape(tokens_b, half_rows),
        ],
        axis=1,
    )
    grad_triple = grad_triple.astype(jnp.bfloat16).reshape(tokens_b, 3 * half_rows)
    grad_hidden_first_sum, grad_triple_all = through_cols(grad_triple, attention_flat, True)
    triple_totals = jnp.sum(grad_triple_all, axis=0, dtype=jnp.float32).reshape(3, half_rows)
    attention_flat_grad, attention_bias_grad = settle(
        weight_gradient(hidden_first_all, grad_triple_all),
        jnp.stack([triple_totals[0], triple_totals[2]]),
    )
    grad_hidden_first = grad_hidden_first_sum.reshape(latents_a, SEQ, half_cols)
    grad_shift_first = jnp.sum(grad_hidden_first, axis=1)
    grad_scale_first = jnp.sum(grad_hidden_first * normed_first, axis=1)
    grad_residual = grad_residual_mid + normalize_back(
        grad_hidden_first * (1.0 + scale_first), normed_first, inverse_first, D
    )
    activations_grad = grad_residual.reshape(tokens_a, half_cols)
    grad_modulation = jnp.stack(
        [
            grad_shift_first,
            grad_scale_first,
            grad_gate_first,
            grad_shift_second,
            grad_scale_second,
            grad_gate_second,
        ],
        axis=1,
    )
    grad_modulation = grad_modulation.astype(jnp.bfloat16).reshape(latents_a, 6 * half_cols)
    grad_silu_sum, grad_modulation_all = through_rows(grad_modulation, modulation_flat, True)
    modulation_flat_grad, modulation_bias_flat = settle(
        weight_gradient(cond_gathered, grad_modulation_all),
        jnp.sum(grad_modulation_all, axis=0, dtype=jnp.float32),
    )
    grad_condition = silu_pullback(grad_silu_sum)[0]
    time_part = table_product(time_onehot.astype(jnp.float32), grad_condition)
    class_part = table_product(class_onehot.astype(jnp.float32), grad_condition)
    time_grad, class_grad = lax.psum((time_part, class_part), ("dp", "col"))
    (
        modulation_flat_grad,
        modulation_bias_flat,
        attention_flat_grad,
        attention_bias_grad,
        projection_grad,
        projection_bias_grad,
        expansion_grad,
        expansion_bias_grad,
        reduction_grad,
        reduction_bias_grad,
    ) = (
        lax.psum(modulation_flat_grad.astype(jnp.bfloat16), "dp").astype(jnp.float32),
        lax.psum(modulation_bias_flat.astype(jnp.bfloat16), "dp").astype(jnp.float32),
        lax.psum(attention_flat_grad.astype(jnp.bfloat16), "dp").astype(jnp.float32),
        lax.psum(attention_bias_grad.astype(jnp.bfloat16), "dp").astype(jnp.float32),
        lax.psum(projection_grad.astype(jnp.bfloat16), "dp").astype(jnp.float32),
        lax.psum(projection_bias_grad.astype(jnp.bfloat16), "dp").astype(jnp.float32),
        lax.psum(expansion_grad.astype(jnp.bfloat16), "dp").astype(jnp.float32),
        lax.psum(expansion_bias_grad.astype(jnp.bfloat16), "dp").astype(jnp.float32),
        lax.psum(reduction_grad.astype(jnp.bfloat16), "dp").astype(jnp.float32),
        lax.psum(reduction_bias_grad.astype(jnp.bfloat16), "dp").astype(jnp.float32),
    )
    return (
        result,
        activations_grad,
        time_grad,
        class_grad,
        modulation_flat_grad.reshape(half_rows, 6, half_cols),
        modulation_bias_flat.reshape(6, half_cols),
        attention_flat_grad.reshape(half_cols, 3, half_rows),
        attention_bias_grad,
        projection_grad,
        projection_bias_grad,
        expansion_grad,
        expansion_bias_grad,
        reduction_grad,
        reduction_bias_grad,
    )


def solution(mesh):
    placed = (
        P(("dp", "row"), "col"),
        P(("dp", "col")),
        P(("dp", "col")),
        P(None, "row"),
        P(None, "row"),
        P("row", None, "col"),
        P(None, "col"),
        P("col", None, "row"),
        P(None, "row"),
        P("row", "col"),
        P("col"),
        P("col", "row"),
        P("row"),
        P("row", "col"),
        P("col"),
        P(("dp", "row"), "col"),
    )
    return jax.shard_map(
        body,
        mesh=mesh,
        in_specs=placed,
        out_specs=(
            P(("dp", "row"), "col"),
            P(("dp", "row"), "col"),
            P(None, "row"),
            P(None, "row"),
            P("row", None, "col"),
            P(None, "col"),
            P("col", None, "row"),
            P(None, "row"),
            P("row", "col"),
            P("col"),
            P("col", "row"),
            P("row"),
            P("row", "col"),
            P("col"),
        ),
        check_vma=False,
    )
```

profile of v0, /device:TPU:0, one launch (start us, length us, event | category | flops | bytes accessed | tf_op | source)
XLA Modules:
  0.0 1217.5 jit_solution(17253089251149624301)
XLA Ops:
  13.2 5.8 all-gather.1
  19.0 2.2 copy.54
  21.2 2.8 copy.53
  24.6 8.4 all-reduce
  35.0 6.4 all-reduce.6
  41.6 6.5 all_gather.31
  48.8 2.2 fusion.45
  51.8 40.4 %reduce-scatter.9.cloned.1.call-done = f32[256,1152]{1,0:T(8,128)} async-done(((f32[512,1152]{1,0:T(8,128)}), f32[256,1152]{1,0:T(8,128)}) %reduce-scatter.9.cloned.1.call-update) | async-done | bytes 1179664 | tf_op jit(solution)/shard_map/reduce_scatter | solution.py:31
  92.2 1.6 copy.55
  95.4 8.8 all_gather.32
  106.6 6.4 all_gather.35
  113.1 4.2 fusion.49
  118.6 6.5 reduce-scatter.11.cloned.1.call-done
  125.1 1.8 fusion.40
  126.8 7.1 all-reduce.5
  136.1 10.5 all_gather.33
  147.3 2.6 fusion.47
  151.4 27.8 %reduce-scatter.17.cloned.1.call-done = f32[256,1536]{1,0:T(8,128)} async-done(((f32[512,1536]{1,0:T(8,128)}), f32[256,1536]{1,0:T(8,128)}) %reduce-scatter.17.cloned.1.call-update) | async-done | bytes 1572880 | tf_op jit(solution)/shard_map/reduce_scatter | solution.py:31
  179.2 49.1 %reduce-scatter.13.cloned.1.call-done = f32[256,1536]{1,0:T(8,128)} async-done(((f32[512,1536]{1,0:T(8,128)}), f32[256,1536]{1,0:T(8,128)}) %reduce-scatter.13.cloned.1.call-update) | async-done | bytes 1572880 | tf_op jit(solution)/shard_map/reduce_scatter | solution.py:31
  228.3 4.2 fusion.6
  233.2 30.2 %all-gather.9.cloned.1.call-done = bf16[512,1536]{1,0:T(8,128)(2,1)} async-done(((bf16[256,1536]{1,0:T(8,128)(2,1)}), bf16[512,1536]{1,0:T(8,128)(2,1)}) %all-gather.9.cloned.1.call-update) | async-done | bytes 1572880 | tf_op jit(solution)/shard_map/all_gather | solution.py:41
  263.3 3.3 fusion.50
  266.7 29.4 %all-gather.7.cloned.1.call-done = bf16[512,1536]{1,0:T(8,128)(2,1)} async-done(((bf16[256,1536]{1,0:T(8,128)(2,1)}), bf16[512,1536]{1,0:T(8,128)(2,1)}) %all-gather.7.cloned.1.call-update) | async-done | bytes 1572880 | tf_op jit(solution)/shard_map/all_gather | solution.py:41
  296.1 3.6 fusion.48
  299.8 18.6 %reduce-scatter.19.cloned.1.call-done = f32[256,384]{1,0:T(8,128)} async-done(((f32[512,384]{1,0:T(8,128)}), f32[256,384]{1,0:T(8,128)}) %reduce-scatter.19.cloned.1.call-update) | async-done | bytes 393232 | tf_op jit(solution)/shard_map/reduce_scatter | solution.py:47
  318.4 1.8 multiply_reduce_fusion.1
  320.3 6.4 all-reduce.4
  326.7 15.8 %reduce-scatter.15.cloned.1.call-done = f32[256,384]{1,0:T(8,128)} async-done(((f32[512,384]{1,0:T(8,128)}), f32[256,384]{1,0:T(8,128)}) %reduce-scatter.15.cloned.1.call-update) | async-done | bytes 393232 | tf_op jit(solution)/shard_map/reduce_scatter | solution.py:47
  342.5 2.8 fusion.14
  346.0 7.3 all_gather.37
  354.9 22.4 %reduce-scatter.21.cloned.1.call-done = f32[256,384]{1,0:T(8,128)} async-done(((f32[512,384]{1,0:T(8,128)}), f32[256,384]{1,0:T(8,128)}) %reduce-scatter.21.cloned.1.call-update) | async-done | bytes 393232 | tf_op jit(solution)/shard_map/reduce_scatter | solution.py:31
  381.9 26.3 %all-gather.11.cloned.1.call-done = bf16[512,1152]{0,1:T(8,128)(2,1)} async-done(((bf16[256,1152]{0,1:T(8,128)(2,1)}), bf16[512,1152]{0,1:T(8,128)(2,1)}) %all-gather.11.cloned.1.call-update) | async-done | bytes 1179664 | tf_op jit(solution)/shard_map/all_gather | solution.py:41
  408.2 3.0 fusion.52
  411.3 3.6 convolution_convert_fusion.1
  414.9 1.8 convolution_convert_fusion.2
  420.0 10.7 reduce-scatter.23.cloned.1.call-done
  432.1 4.4 all-gather.2
  437.1 2.2 copy.61
  441.2 6.5 all-reduce.3
  452.8 1.5 reduce.38
  454.4 126.8 %all-reduce.7 = (bf16[6,384]{1,0:T(8,128)(2,1)S(1)}, bf16[2,384]{1,0:T(2,128)(2,1)S(1)}, bf16[384]{0:T(512)(128)(2,1)S(1)}, bf16[1536]{0:T(1024)(128)(2,1)S(1)}, bf16[384]{0:T(512)(128)(2,1)S(1)}) all-reduce(bf16[6,384]{1,0:T(8,128)(2,1)S(1)} %reshape.419, ...), channel_id=1, replica_groups=mesh['dp'=32,'row'=2,'col'=2] {'dp'}, use_global_device_ids=true, to_apply=%region_39.40 | all-reduce | flops 5376 | bytes 21504 | tf_op jit(solution)/shard_map/psum | solution.py:305
  585.1 1.8 convert_element_type.208
  586.9 4.1 copy.63
  591.1 2.4 copy.64
  593.5 1.7 convert_element_type.211
  595.2 1.6 convert_element_type.214
  596.7 610.3 %all-reduce.12.cloned.1.call-done = (f32[1000,384]{1,0:T(8,128)}, f32[1001,384]{1,0:T(8,128)}) async-done(((f32[1000,384]{1,0:T(8,128)}, f32[1001,384]{1,0:T(8,128)}), (f32[1000,384]{1,0:T(8,128)}, f32[1001,384]{1,0:T(8,128)})) %all-reduce.12.cloned.1.call-update) | async-done | bytes 3073552 | tf_op jit(solution)/shard_map/psum | solution.py:291
  1207.0 2.8 copy.96
  (236 shorter events, 43.0 us)
Async XLA Ops:
  7.2 140.2 %copy-start = (bf16[384,1536]{1,0:T(8,128)(2,1)S(1)}, bf16[384,1536]{1,0:T(8,128)(2,1)}, u32[]{:S(2)}) copy-start(bf16[384,1536]{1,0:T(8,128)(2,1)} %param.27) | copy-start | bytes 3538948
  7.2 11.8 copy-start.29
  7.2 85.0 %reduce-scatter.9.cloned.1.call-start = ((), (), s32[]{:S(2)}) async-start(), calls=%async_computation.8 | async-start | bytes 3538944 | tf_op jit(solution)/shard_map/reduce_scatter | solution.py:31
  13.2 8.0 copy-start.36
  13.2 8.0 copy-start.38
  19.0 5.0 copy-start.50
  24.0 27.1 %copy-start.2 = (bf16[384,6,384]{0,2,1:T(8,128)(2,1)}, bf16[384,6,384]{0,2,1:T(8,128)(2,1)S(1)}, u32[]{:S(2)}) copy-start(bf16[384,6,384]{0,2,1:T(8,128)(2,1)S(1)} %copy.53) | copy-start | bytes 5308420
  24.0 9.1 copy-start.62
  24.0 10.3 copy-start.54
  24.0 17.4 %copy-start.4 = (bf16[256,384]{1,0:T(8,128)(2,1)S(1)}, bf16[256,384]{1,0:T(8,128)(2,1)}, u32[]{:S(2)}) copy-start(bf16[256,384]{1,0:T(8,128)(2,1)} %param.16) | copy-start | bytes 589828
  41.4 7.4 copy-start.5
  41.4 9.6 copy-start.46
  41.4 9.6 copy-start.48
  51.1 74.0 %reduce-scatter.11.cloned.1.call-start = ((), (), s32[]{:S(2)}) async-start(), calls=%async_computation.9 | async-start | bytes 1179648 | tf_op jit(solution)/shard_map/reduce_scatter | solution.py:47
  94.9 9.4 copy-start.27
  105.6 73.6 %reduce-scatter.17.cloned.1.call-start = ((), (), s32[]{:S(2)}) async-start(), calls=%async_computation.13 | async-start | bytes 4718592 | tf_op jit(solution)/shard_map/reduce_scatter | solution.py:31
  113.1 4.2 copy-start.7
  117.3 111.0 %reduce-scatter.13.cloned.1.call-start = ((), (), s32[]{:S(2)}) async-start(), calls=%async_computation.10 | async-start | bytes 4718592 | tf_op jit(solution)/shard_map/reduce_scatter | solution.py:31
  150.0 113.3 %all-gather.9.cloned.1.call-start = ((), (), s32[]{:S(2)}) async-start(), calls=%async_computation.14 | async-start | bytes 2359296 | tf_op jit(solution)/shard_map/all_gather | solution.py:41
  232.5 63.6 %all-gather.7.cloned.1.call-start = ((), (), s32[]{:S(2)}) async-start(), calls=%async_computation.11 | async-start | bytes 2359296 | tf_op jit(solution)/shard_map/all_gather | solution.py:41
  233.1 85.3 %reduce-scatter.19.cloned.1.call-start = ((), (), s32[]{:S(2)}) async-start(), calls=%async_computation.15 | async-start | bytes 1179648 | tf_op jit(solution)/shard_map/reduce_scatter | solution.py:47
  266.7 33.2 %copy-start.60 = (bf16[384]{0:T(512)(128)(2,1)S(1)}, bf16[384]{0:T(512)(128)(2,1)}, u32[]{:S(2)}) copy-start(bf16[384]{0:T(512)(128)(2,1)} %param.30) | copy-start | bytes 2308
  266.7 51.8 %copy-start.43 = (f32[1,256]{1,0:T(1,128)S(1)}, f32[1,256]{1,0:T(1,128)}, u32[]{:S(2)}) copy-start(f32[1,256]{1,0:T(1,128)} %copy-done.42) | copy-start | bytes 3076
  266.7 51.8 %copy-start.45 = (f32[1,256]{1,0:T(1,128)S(1)}, f32[1,256]{1,0:T(1,128)}, u32[]{:S(2)}) copy-start(f32[1,256]{1,0:T(1,128)} %copy-done.44) | copy-start | bytes 3076
  266.7 75.8 %reduce-scatter.15.cloned.1.call-start = ((), (), s32[]{:S(2)}) async-start(), calls=%async_computation.12 | async-start | bytes 1179648 | tf_op jit(solution)/shard_map/reduce_scatter | solution.py:47
  299.7 42.7 %copy-start.22 = (f32[256,384]{1,0:T(8,128)S(1)}, f32[256,384]{1,0:T(8,128)}, u32[]{:S(2)}) copy-start(f32[256,384]{1,0:T(8,128)} %reduce-scatter.11.cloned.1.call-done) | copy-start | bytes 1179652
  299.7 42.7 %copy-start.40 = (f32[384]{0:T(512)S(1)}, f32[384]{0:T(512)}, u32[]{:S(2)}) copy-start(f32[384]{0:T(512)} %convert_element_type.188) | copy-start | bytes 4612
  299.7 42.7 %copy-start.41 = (f32[384]{0:T(512)S(1)}, f32[384]{0:T(512)}, u32[]{:S(2)}) copy-start(f32[384]{0:T(512)} %get-tuple-element.54) | copy-start | bytes 4612
  299.8 77.5 %reduce-scatter.21.cloned.1.call-start = ((), (), s32[]{:S(2)}) async-start(), calls=%async_computation.16 | async-start | bytes 1179648 | tf_op jit(solution)/shard_map/reduce_scatter | solution.py:31
  299.8 46.2 %copy-start.35 = (f32[384]{0:T(512)S(1)}, f32[384]{0:T(512)}, u32[]{:S(2)}) copy-start(f32[384]{0:T(512)} %get-tuple-element.59) | copy-start | bytes 4612
  342.5 10.9 copy-start.28
  346.0 8.9 copy-start.34
  354.7 24.2 %copy-start.32 = (bf16[256,1,384]{0,2,1:T(8,128)(2,1)S(1)}, bf16[256,1,384]{0,2,1:T(8,128)(2,1)}, u32[]{:S(2)}) copy-start(bf16[256,1,384]{0,2,1:T(8,128)(2,1)} %copy-done.31) | copy-start | bytes 589828
  354.7 53.5 %all-gather.11.cloned.1.call-start = ((), (), s32[]{:S(2)}) async-start(), calls=%async_computation.17 | async-start | bytes 1769472 | tf_op jit(solution)/shard_map/all_gather | solution.py:41
  380.6 27.5 %copy-start.6 = (bf16[384,3,384]{0,2,1:T(8,128)(2,1)S(1)}, bf16[384,3,384]{0,2,1:T(8,128)(2,1)}, u32[]{:S(2)}) copy-start(bf16[384,3,384]{0,2,1:T(8,128)(2,1)} %copy.54) | copy-start | bytes 2654212
  381.8 29.5 %copy-start.8 = (bf16[512,384]{1,0:T(8,128)(2,1)S(1)}, bf16[512,384]{1,0:T(8,128)(2,1)}, u32[]{:S(2)}) copy-start(bf16[512,384]{1,0:T(8,128)(2,1)} %copy-done.7) | copy-start | bytes 1179652
  381.8 48.9 %reduce-scatter.23.cloned.1.call-start = ((), (), s32[]{:S(2)}) async-start(), calls=%async_computation.18 | async-start | bytes 1179648 | tf_op jit(solution)/shard_map/reduce_scatter | solution.py:47
  411.2 173.9 %all-reduce.14.cloned.1.call-start = ((), (), s32[]{:S(2)}) async-start(), calls=%async_computation.20 | async-start | bytes 10616832 | tf_op jit(solution)/shard_map/psum | solution.py:304
  417.9 12.8 %copy-start.47 = (f32[1,256]{1,0:T(1,128)S(1)}, f32[1,256]{1,0:T(1,128)}, u32[]{:S(2)}) copy-start(f32[1,256]{1,0:T(1,128)} %copy-done.46) | copy-start | bytes 3076
  417.9 12.8 %copy-start.49 = (f32[1,256]{1,0:T(1,128)S(1)}, f32[1,256]{1,0:T(1,128)}, u32[]{:S(2)}) copy-start(f32[1,256]{1,0:T(1,128)} %copy-done.48) | copy-start | bytes 3076
  418.6 17.8 %copy-start.51 = (bf16[2,1,384]{2,1,0:T(2,128)(2,1)S(1)}, bf16[2,1,384]{2,1,0:T(2,128)(2,1)}, u32[]{:S(2)}) copy-start(bf16[2,1,384]{2,1,0:T(2,128)(2,1)} %copy-done.50) | copy-start | bytes 4612
  439.4 8.3 copy-start.37
  439.4 8.3 copy-start.39
  439.4 8.3 copy-start.52
  439.4 767.6 %all-reduce.12.cloned.1.call-start = ((), (), s32[]{:S(2)}) async-start(), calls=%async_computation.19 | async-start | bytes 6168576 | tf_op jit(solution)/shard_map/psum | solution.py:291
  452.4 131.8 %copy-start.12 = (f32[256,384]{1,0:T(8,128)S(1)}, f32[256,384]{1,0:T(8,128)}, u32[]{:S(2)}) copy-start(f32[256,384]{1,0:T(8,128)} %copy-done.11) | copy-start | bytes 1179652
  452.4 131.8 %copy-start.21 = (f32[256,384]{1,0:T(8,128)S(1)}, f32[256,384]{1,0:T(8,128)}, u32[]{:S(2)}) copy-start(f32[256,384]{1,0:T(8,128)} %reduce-scatter.23.cloned.1.call-done) | copy-start | bytes 1179652
  586.9 4.1 copy-start.30
  (28 other events, 47.0 us)
Sparse Core Ops, SparseCore 0:
  51.2 40.9 reduce-scatter.8
  105.7 19.3 reduce-scatter.10
  128.0 51.0 reduce-scatter.16
  181.5 46.7 reduce-scatter.12
  232.6 30.6 all-gather.8
  265.4 30.6 all-gather.6
  299.0 19.3 reduce-scatter.18
  321.5 20.9 reduce-scatter.14
  354.8 22.4 reduce-scatter.20
  381.9 26.1 all-gather.10
  411.3 19.3 reduce-scatter.22
  439.5 115.9 all-reduce.13
  558.8 648.1 all-reduce.11
where the time goes:
time: 1220 us
  waiting for transfers between devices  888 us (73%)
  blocking collectives  211 us (17%)
  other arithmetic  36 us (3%)
  matrix products  35.4 us (3%)
  local copies, waits for them, and re-layouts  29.8 us (2%)
  between operations  16.1 us (1%)
    psum x1, waiting for transfers between devices, body(): time_grad, class_grad = lax.psum((time_part, class_part), ('dp', 'col'))  610 us
    reduce_scatter x4, waiting for transfers between devices, through_rows(): lax.psum_scatter(row_term(jnp.int32(0), keep_rows * lax.axis_size('col'))...  140 us
    psum x1, blocking collectives, body(): lax.psum(modulation_bias_flat.astype(jnp.bfloat16), 'dp')  127 us
    all_gather x3, waiting for transfers between devices, through_cols(): gathered = lax.all_gather(local_rows, 'col', axis=0, tiled=True)  85.9 us
    reduce_scatter x4, waiting for transfers between devices, through_cols(): lax.psum_scatter(row_term(jnp.int32(0), keep_rows * lax.axis_size('row'))...  51.6 us
    all_gather x5, blocking collectives, through_rows(): gathered = lax.all_gather(local_rows, 'row', axis=0, tiled=True)  35.1 us
    psum x4, blocking collectives, column_totals(): lax.psum((jnp.sum(first_terms, axis=-1), jnp.sum(second_terms, axis=-1)),...  26.4 us
  transfers between devices with their start and end apart: 13, of which 12 were waited for; matrix products, arithmetic and copies ran while one was open for 4% of the time, Pallas kernels for 0%

commit v1 on v0

v1 whole, which is shorter than its diff:
```python
import math

import jax
import jax.numpy as jnp
from jax import lax
from jax.experimental import pallas as pl
from jax.experimental.pallas import tpu as pltpu
from jax.sharding import PartitionSpec as P

D = 768
HALF = 384
SEQ = 256
HEAD_DIM = 64
STEPS = 1000
CLASSES = 1001
SEG = 1536
EPSILON = 1e-06
ROWS = 32
SEMS = 128
F32 = jnp.float32
BF16 = jnp.bfloat16
MESH = pl.DeviceIdType.MESH


def dot(u, v):
    return lax.dot_general(u, v, (((1,), (0,)), ((), ())), preferred_element_type=F32)


def dot_nt(u, v):
    return lax.dot_general(u, v, (((1,), (1,)), ((), ())), preferred_element_type=F32)


def dot_tn(u, v):
    return lax.dot_general(u, v, (((0,), (0,)), ((), ())), preferred_element_type=F32)


def xor(u, v):
    return u + v - 2 * u * v


class Place:
    def __init__(self, n):
        self.n = n
        self.dp = lax.axis_index("dp")
        self.r = lax.axis_index("row")
        self.c = lax.axis_index("col")
        self.k = lax.rem(self.dp, 2)
        chip = lax.div(self.dp, 2)
        z = lax.rem(chip, n)
        x = lax.div(chip, n)
        self.major = x * (1 - self.k) + z * self.k
        self.minor = z * (1 - self.k) + x * self.k
        self.shard = (self.k * n + self.major) * n + self.minor
        self.latent = xor(self.c, self.k * self.r)

    def at(self, dp=None, row=None, col=None):
        return {
            "dp": self.dp if dp is None else dp,
            "row": self.r if row is None else row,
            "col": self.c if col is None else col,
        }

    def plane(self, major, minor):
        x = major * (1 - self.k) + minor * self.k
        z = minor * (1 - self.k) + major * self.k
        return self.at(dp=(x * self.n + z) * 2 + self.k)

    def along_minor(self, step):
        return self.plane(self.major, lax.rem(self.minor + step, self.n))

    def along_major(self, step):
        return self.plane(lax.rem(self.major + step, self.n), self.minor)

    def sibling(self):
        return self.at(dp=self.dp + 1 - 2 * self.k)

    def group(self, step):
        row = xor(self.r, step & 1)
        col = xor(self.c, step >> 1)
        return self.at(row=row, col=col)

    def partner(self):
        return self.at(row=1 - self.r, col=xor(self.c, self.k))

    def column(self):
        return self.at(col=1 - self.c)


class Wires:
    def __init__(self, send_sems, recv_sems):
        self.send_sems, self.recv_sems = send_sems, recv_sems
        self.used = 0
        self.sent = []

    def slot(self):
        self.used += 1
        assert self.used <= SEMS
        return self.used - 1

    def copy(self, slot, src, dst, device):
        return pltpu.make_async_remote_copy(
            src_ref=src,
            dst_ref=dst,
            send_sem=self.send_sems.at[slot],
            recv_sem=self.recv_sems.at[slot],
            device_id=device,
            device_id_type=MESH,
        )

    def send(self, slot, src, dst, device):
        copy = self.copy(slot, src, dst, device)
        copy.start()
        self.sent.append(copy)

    def arrived(self, slot, dst, device):
        self.copy(slot, dst, dst, device).wait_recv()

    def drain(self):
        for copy in self.sent:
            copy.wait_send()


class Gather:
    def __init__(self, place, wires, view):
        self.place, self.wires, self.view = place, wires, view
        self.slots = [wires.slot() for _ in range(2 * (place.n - 1) + 1)]

    def minor(self):
        p, w, n = self.place, self.wires, self.place.n
        mine = self.view(p.shard, 1)
        for step in range(1, n):
            w.send(self.slots[step - 1], mine, mine, p.along_minor(step))

    def major(self):
        p, w, n = self.place, self.wires, self.place.n
        row = (p.k * n + p.major) * n
        for step in range(1, n):
            other = lax.rem(p.minor + n - step, n)
            w.arrived(self.slots[step - 1], self.view(row + other, 1), p.along_minor(step))
        mine = self.view(row, n)
        for step in range(1, n):
            w.send(self.slots[n - 2 + step], mine, mine, p.along_major(step))

    def cores(self):
        p, w, n = self.place, self.wires, self.place.n
        for step in range(1, n):
            other = lax.rem(p.major + n - step, n)
            block = self.view((p.k * n + other) * n, n)
            w.arrived(self.slots[n - 2 + step], block, p.along_major(step))
        mine = self.view(p.k * n * n, n * n)
        w.send(self.slots[-1], mine, mine, p.sibling())

    def finish(self):
        p, w, n = self.place, self.wires, self.place.n
        w.arrived(self.slots[-1], self.view((1 - p.k) * n * n, n * n), p.sibling())


class Reduce:
    def __init__(self, place, wires, seg, grads, from_core, from_major, from_minor, from_col, final):
        self.place, self.wires, self.seg = place, wires, seg
        self.grads, self.final = grads, final
        self.from_core, self.from_major = from_core, from_major
        self.from_minor, self.from_col = from_minor, from_col
        n = place.n
        self.rows = SEG // (2 * n * n)
        self.slots = [wires.slot() for _ in range(2 * n)]
        self.gather = Gather(place, wires, self.final_view)

    def view(self, first, count):
        start = pl.multiple_of(first * self.rows, 16)
        return self.grads.at[self.seg, :, pl.ds(start, count * self.rows)]

    def final_view(self, first, count):
        start = pl.multiple_of(first * self.rows, 16)
        return self.final.at[self.seg, pl.ds(start, count * self.rows)]

    def add(self, first, count, arrivals):
        chunk = 48
        base = first * self.rows

        def step(i, carry):
            at = pl.ds(pl.multiple_of(base + i * chunk, 16), chunk)
            here = pl.ds(pl.multiple_of(i * chunk, 16), chunk)
            total = self.grads[self.seg, :, at].astype(F32)
            for ref in arrivals:
                total = total + ref[:, here].astype(F32)
            self.grads[self.seg, :, at] = total.astype(BF16)
            return carry

        lax.fori_loop(0, count * self.rows // chunk, step, 0)

    def to_core(self):
        p, n = self.place, self.place.n
        self.wires.send(
            self.slots[0],
            self.view((1 - p.k) * n * n, n * n),
            self.from_core.at[self.seg],
            p.sibling(),
        )

    def to_major(self):
        p, w, n = self.place, self.wires, self.place.n
        w.arrived(self.slots[0], self.from_core.at[self.seg], p.sibling())
        self.add(p.k * n * n, n * n, [self.from_core.at[self.seg]])
        for step in range(1, n):
            other = lax.rem(p.major + step, n)
            w.send(
                self.slots[step],
                self.view((p.k * n + other) * n, n),
                self.from_major.at[self.seg, step - 1],
                p.along_major(step),
            )

    def to_minor(self):
        p, w, n = self.place, self.wires, self.place.n
        for step in range(1, n):
            w.arrived(self.slots[step], self.from_major.at[self.seg, step - 1], p.along_major(step))
        row = (p.k * n + p.major) * n
        if n > 1:
            self.add(row, n, [self.from_major.at[self.seg, step - 1] for step in range(1, n)])
        for step in range(1, n):
            other = lax.rem(p.minor + step, n)
            w.send(
                self.slots[n - 1 + step],
                self.view(row + other, 1),
                self.from_minor.at[self.seg, step - 1],
                p.along_minor(step),
            )

    def to_col(self):
        p, w, n = self.place, self.wires, self.place.n
        for step in range(1, n):
            w.arrived(
                self.slots[n - 1 + step], self.from_minor.at[self.seg, step - 1], p.along_minor(step)
            )
        if n > 1:
            self.add(p.shard, 1, [self.from_minor.at[self.seg, step - 1] for step in range(1, n)])
        start = pl.multiple_of(p.shard * self.rows, 16)
        w.send(
            self.slots[-1],
            self.grads.at[self.seg, 1 - p.c, pl.ds(start, self.rows)],
            self.from_col.at[self.seg],
            p.column(),
        )

    def to_gather(self):
        p, w = self.place, self.wires
        w.arrived(self.slots[-1], self.from_col.at[self.seg], p.column())
        start = pl.multiple_of(p.shard * self.rows, 16)
        mine = self.grads[self.seg, p.c, pl.ds(start, self.rows)].astype(F32)
        total = mine + self.from_col[self.seg].astype(F32)
        self.final[self.seg, pl.ds(start, self.rows)] = total.astype(BF16)
        self.gather.minor()


def kernel(
    n,
    x_ref,
    cot_ref,
    modp_ref,
    weights_hbm,
    triple_bias_ref,
    widening_ref,
    result_ref,
    xgrad_ref,
    final_hbm,
    payload_hbm,
    weights,
    x_all,
    cot_all,
    mod_parts,
    mod,
    normed1,
    rstd1,
    hidden1,
    triple,
    probs,
    attended,
    send1,
    recv1,
    branch1,
    normed2,
    rstd2,
    hidden2,
    activated,
    slope,
    grad_b2,
    send2,
    recv2,
    grad_up,
    send3,
    recv3,
    grad_res,
    grad_b1,
    grad_att,
    grad_tri,
    send4,
    recv4,
    res_out,
    res_in,
    xg_out,
    xg_in,
    payload_out,
    payload,
    grads,
    from_core,
    from_major,
    from_minor,
    from_col,
    final,
    send_sems,
    recv_sems,
    local_sems,
):
    place = Place(n)
    wires = Wires(send_sems, recv_sems)
    r, c, k, latent = place.r, place.c, place.k, place.latent

    barrier = pltpu.get_barrier_semaphore()
    others = [place.group(s) for s in (1, 2, 3)] + [place.sibling()]
    for step in range(1, n):
        others += [place.along_minor(step), place.along_major(step)]
    for other in others:
        pl.semaphore_signal(barrier, inc=1, device_id=other, device_id_type=MESH)
    pl.semaphore_wait(barrier, len(others))

    shard_rows = SEG // (2 * n * n)

    def weight_view(seg):
        def view(first, count):
            start = pl.multiple_of(first * shard_rows, 16)
            return weights.at[seg, 1 - c, pl.ds(start, count * shard_rows)]

        return view

    gathers = [Gather(place, wires, weight_view(seg)) for seg in range(3)]
    weight_slots = [wires.slot() for _ in range(3)]
    my_rows = pl.ds(pl.multiple_of(place.shard * shard_rows, 16), shard_rows)

    def weights_out(seg):
        wires.send(
            weight_slots[seg],
            weights_hbm.at[seg, my_rows],
            weights.at[seg, c, my_rows],
            place.column(),
        )

    def weights_minor(seg):
        wires.arrived(weight_slots[seg], weights.at[seg, 1 - c, my_rows], place.column())
        gathers[seg].minor()

    own = [
        pltpu.make_async_copy(weights_hbm.at[seg], weights.at[seg, c], local_sems.at[seg])
        for seg in range(3)
    ]

    weights_out(0)
    own[0].start()
    own[1].start()
    own[2].start()
    mod_slots = [wires.slot() for _ in range(3)]
    for step in (1, 2, 3):
        there = place.group(step)
        its_latent = xor(there["col"], k * there["row"])
        wires.send(
            mod_slots[step - 1], modp_ref.at[its_latent], mod_parts.at[step], there
        )
    _, x_collect, x_sent = spread_halves(place, wires, x_ref, x_all)
    weights_out(1)
    weights_out(2)
    _, cot_collect, cot_sent = spread_halves(place, wires, cot_ref, cot_all)
    weights_minor(0)

    for step in (1, 2, 3):
        wires.arrived(mod_slots[step - 1], mod_parts.at[step], place.group(step))
    mod[c] = modp_ref[latent] + mod_parts[1]
    mod[1 - c] = mod_parts[2] + mod_parts[3]

    def vec(half, row):
        return mod[half, row : row + 1, :]

    def over_rows(body, init=0):
        def step(i, carry):
            return body(pl.ds(pl.multiple_of(i * ROWS, ROWS), ROWS), carry)

        return lax.fori_loop(0, SEQ // ROWS, step, init)

    def norm(values):
        average = (
            jnp.sum(values[0], axis=-1, keepdims=True) + jnp.sum(values[1], axis=-1, keepdims=True)
        ) * (1.0 / D)
        square = (
            jnp.sum(values[0] * values[0], axis=-1, keepdims=True)
            + jnp.sum(values[1] * values[1], axis=-1, keepdims=True)
        ) * (1.0 / D)
        inverse = lax.rsqrt(square - average * average + EPSILON)
        return [(v - average) * inverse for v in values], inverse

    def norm_back(grad, normed, inverse):
        average = (
            jnp.sum(grad[0], axis=-1, keepdims=True) + jnp.sum(grad[1], axis=-1, keepdims=True)
        ) * (1.0 / D)
        crossed = (
            jnp.sum(grad[0] * normed[0], axis=-1, keepdims=True)
            + jnp.sum(grad[1] * normed[1], axis=-1, keepdims=True)
        ) * (1.0 / D)
        return [inverse * (g - average - m * crossed) for g, m in zip(grad, normed)]

    def token_sum(v):
        return jnp.sum(v, axis=0, keepdims=True)

    x_collect()
    gathers[0].major()

    def first_norm(rows, carry):
        normed, inverse = norm([x_all[h, rows].astype(F32) for h in range(2)])
        rstd1[rows] = inverse
        for h in range(2):
            normed1[h, rows] = normed[h]
            hidden1[h, rows] = (normed[h] * (1.0 + vec(h, 1)) + vec(h, 0)).astype(BF16)
        return carry

    over_rows(first_norm)
    gathers[0].cores()
    weights_minor(1)
    weights_minor(2)
    own[0].wait()
    gathers[0].finish()

    def weight(seg, half, block):
        return weights[seg, half, block * HALF : (block + 1) * HALF, :]

    for kind in range(3):
        value = dot(hidden1[0], weight(0, 0, kind)) + dot(hidden1[1], weight(0, 1, kind))
        triple[kind] = (value + triple_bias_ref[kind]).astype(BF16)
    gathers[1].major()

    low_lanes = lax.broadcasted_iota(jnp.int32, (SEQ, 128), 1) < HEAD_DIM

    def one_head(v, head):
        mask = low_lanes if head == 0 else jnp.logical_not(low_lanes)
        return jnp.where(mask, v, jnp.zeros_like(v))

    score_scale = HEAD_DIM ** (-0.5)

    def attend(pair, carry):
        lanes = pl.ds(pl.multiple_of(pair * 128, 128), 128)
        query = triple[0, :, lanes] * BF16(score_scale)
        keys = triple[1, :, lanes]
        values = triple[2, :, lanes]
        mixed = []
        for head in range(2):
            scores = dot_nt(one_head(query, head), keys)
            exponent = jnp.exp(scores - jnp.max(scores, axis=-1, keepdims=True))
            total = jnp.sum(exponent, axis=-1, keepdims=True)
            weights_now = exponent * (1.0 / total)
            probs[2 * pair + head] = weights_now
            mixed.append(dot(weights_now.astype(BF16), values))
        attended[:, lanes] = jnp.where(low_lanes, mixed[0], mixed[1]).astype(BF16)
        return carry

    lax.fori_loop(0, 3, attend, 0)
    gathers[1].cores()
    gathers[2].major()

    def exchange(half, value, out, landing, slots):
        out[half] = value.astype(BF16)
        wires.send(slots[half], out.at[half], landing.at[half], place.partner())

    def exchanged(landing, slots):
        for half in range(2):
            wires.arrived(slots[half], landing.at[half], place.partner())

    slots1, slots2, slots3, slots4 = ([wires.slot() for _ in range(2)] for _ in range(4))
    for half in range(2):
        exchange(half, dot(attended[...], weight(0, half, 3)), send1, recv1, slots1)
    cot_collect()
    zero = jnp.zeros((1, HALF), F32)

    def start_back(rows, carry):
        out = []
        for h in range(2):
            low = (cot_all[h, rows].astype(F32) * vec(h, 5)).astype(BF16)
            grad_b2[h, rows] = low
            out.append(carry[h] + token_sum(low.astype(F32)))
        return tuple(out)

    narrowing_sum = over_rows(start_back, (zero, zero))
    gathers[2].cores()
    exchanged(recv1, slots1)

    def second_norm(rows, carry):
        middle = []
        for h in range(2):
            branch = send1[h, rows].astype(F32) + recv1[h, rows].astype(F32) + vec(h, 6)
            branch1[h, rows] = branch
            middle.append(x_all[h, rows].astype(F32) + vec(h, 2) * branch)
        normed, inverse = norm(middle)
        rstd2[rows] = inverse
        for h in range(2):
            normed2[h, rows] = normed[h]
            hidden2[h, rows] = (normed[h] * (1.0 + vec(h, 4)) + vec(h, 3)).astype(BF16)
        return carry

    over_rows(second_norm)
    own[1].wait()
    gathers[1].finish()
    root = math.sqrt(2.0 / math.pi)
    for block in range(4):
        upper = dot(hidden2[0], weight(1, 0, block)) + dot(hidden2[1], weight(1, 1, block))
        upper = upper + widening_ref[block]
        squared = upper * upper
        bent = jnp.tanh(root * upper * (1.0 + 0.044715 * squared))
        half_up = 0.5 * (1.0 + bent)
        activated[block] = (upper * half_up).astype(BF16)
        slope[block] = half_up + (0.5 * root) * upper * (1.0 - bent * bent) * (
            1.0 + (3.0 * 0.044715) * squared
        )
    own[2].wait()
    gathers[2].finish()
    widening_sum = []
    for block in range(4):
        back = dot_nt(grad_b2[0], weight(2, 0, block)) + dot_nt(grad_b2[1], weight(2, 1, block))
        low = (back * slope[block]).astype(BF16)
        grad_up[block] = low
        widening_sum.append(token_sum(low.astype(F32)))
    for half in range(2):
        value = dot_nt(grad_up[0], weight(1, half, 0))
        for block in range(1, 4):
            value = value + dot_nt(grad_up[block], weight(1, half, block))
        exchange(half, value, send3, recv3, slots3)
    for half in range(2):
        value = dot(activated[0], weight(2, half, 0))
        for block in range(1, 4):
            value = value + dot(activated[block], weight(2, half, block))
        exchange(half, value, send2, recv2, slots2)

    reduces = [
        Reduce(place, wires, seg, grads, from_core, from_major, from_minor, from_col, final)
        for seg in range(3)
    ]

    def keep_grad(seg, half, block, value):
        grads[seg, half, block * HALF : (block + 1) * HALF, :] = value.astype(BF16)

    for block in range(4):
        for half in range(2):
            keep_grad(2, half, block, dot_tn(activated[block], grad_b2[half]))
    reduces[2].to_core()
    for block in range(4):
        for half in range(2):
            keep_grad(1, half, block, dot_tn(hidden2[half], grad_up[block]))
    reduces[1].to_core()

    exchanged(recv3, slots3)

    def second_back(rows, carry):
        shift, scale, gate, bias = (list(part) for part in carry)
        inverse = rstd2[rows]
        normed = [normed2[h, rows] for h in range(2)]
        scaled = []
        for h in range(2):
            grad = send3[h, rows].astype(F32) + recv3[h, rows].astype(F32)
            shift[h] = shift[h] + token_sum(grad)
            scale[h] = scale[h] + token_sum(grad * normed[h])
            scaled.append(grad * (1.0 + vec(h, 4)))
        back = norm_back(scaled, normed, inverse)
        for h in range(2):
            total = cot_all[h, rows].astype(F32) + back[h]
            grad_res[h, rows] = total
            gate[h] = gate[h] + token_sum(total * branch1[h, rows])
            low = (total * vec(h, 2)).astype(BF16)
            grad_b1[h, rows] = low
            bias[h] = bias[h] + token_sum(low.astype(F32))
        return tuple(shift), tuple(scale), tuple(gate), tuple(bias)

    pair_zero = (zero, zero)
    shift2, scale2, gate1, projection_sum = over_rows(second_back, (pair_zero,) * 4)
    grad_att[...] = (
        dot_nt(grad_b1[0], weight(0, 0, 3)) + dot_nt(grad_b1[1], weight(0, 1, 3))
    ).astype(BF16)
    reduces[2].to_major()
    for half in range(2):
        keep_grad(0, half, 3, dot_tn(attended[...], grad_b1[half]))

    def attend_back(pair, carry):
        lanes = pl.ds(pl.multiple_of(pair * 128, 128), 128)
        query = triple[0, :, lanes] * BF16(score_scale)
        keys = triple[1, :, lanes]
        values = triple[2, :, lanes]
        above = grad_att[:, lanes]
        by_query, by_keys, by_values = [], [], []
        for head in range(2):
            weights_now = probs[2 * pair + head]
            grad_probs = dot_nt(one_head(above, head), values)
            by_values.append(dot_tn(weights_now.astype(BF16), above))
            crossed = jnp.sum(grad_probs * weights_now, axis=-1, keepdims=True)
            low = (weights_now * (grad_probs - crossed)).astype(BF16)
            by_query.append(dot(low, keys) * score_scale)
            by_keys.append(dot_tn(low, query))
        for kind, parts in enumerate((by_query, by_keys, by_values)):
            grad_tri[kind, :, lanes] = jnp.where(low_lanes, parts[0], parts[1]).astype(BF16)
        return carry

    lax.fori_loop(0, 3, attend_back, 0)
    for half in range(2):
        value = dot_nt(grad_tri[0], weight(0, half, 0))
        for kind in range(1, 3):
            value = value + dot_nt(grad_tri[kind], weight(0, half, kind))
        exchange(half, value, send4, recv4, slots4)
    reduces[1].to_major()
    for half in range(2):
        for kind in range(3):
            keep_grad(0, half, kind, dot_tn(hidden1[half], grad_tri[kind]))
    reduces[0].to_core()
    reduces[2].to_minor()

    exchanged(recv2, slots2)
    mine = r == latent
    self_col = xor(latent, k * latent)
    out_half = c * (r == latent).astype(jnp.int32) + (1 - self_col) * (r != latent).astype(jnp.int32)
    across = place.at(row=latent, col=1 - self_col)
    back_from = place.at(row=1 - r, col=xor(r, k * (1 - r)))

    def branch_end(rows, carry):
        gate = list(carry)
        for h in range(2):
            branch = send2[h, rows].astype(F32) + recv2[h, rows].astype(F32) + vec(h, 7)
            gate[h] = gate[h] + token_sum(cot_all[h, rows].astype(F32) * branch)
            middle = x_all[h, rows].astype(F32) + vec(h, 2) * branch1[h, rows]
            res_out[h, rows] = (middle + vec(h, 5) * branch).astype(BF16)
        return tuple(gate)

    gate2 = over_rows(branch_end, pair_zero)
    res_slot, xg_slot = wires.slot(), wires.slot()

    @pl.when(jnp.logical_not(mine))
    def _():
        wires.copy(res_slot, res_out.at[out_half], res_in, across).start()

    reduces[1].to_minor()
    reduces[2].to_col()
    exchanged(recv4, slots4)

    def first_back(rows, carry):
        shift, scale = (list(part) for part in carry)
        inverse = rstd1[rows]
        normed = [normed1[h, rows] for h in range(2)]
        scaled = []
        for h in range(2):
            grad = send4[h, rows].astype(F32) + recv4[h, rows].astype(F32)
            shift[h] = shift[h] + token_sum(grad)
            scale[h] = scale[h] + token_sum(grad * normed[h])
            scaled.append(grad * (1.0 + vec(h, 1)))
        back = norm_back(scaled, normed, inverse)
        for h in range(2):
            xg_out[h, rows] = grad_res[h, rows] + back[h]
        return tuple(shift), tuple(scale)

    shift1, scale1 = over_rows(first_back, (pair_zero,) * 2)

    def sums(kind):
        return token_sum(grad_tri[kind].astype(F32))

    shared = [sums(0), sums(2)] + widening_sum + [jnp.zeros((2, HALF), F32)]
    for h in range(2):
        own_rows = [shift1[h], scale1[h], gate1[h], shift2[h], scale2[h], gate2[h]]
        own_rows += [projection_sum[h], narrowing_sum[h]]
        payload_out[h] = jnp.concatenate(own_rows + shared, axis=0).astype(BF16)
    payload_slot = wires.slot()
    spot = 2 * place.shard + latent
    wires.send(payload_slot, payload_out.at[1 - c], payload.at[spot], place.column())
    payload[spot] = payload_out[c]

    @pl.when(jnp.logical_not(mine))
    def _():
        wires.copy(xg_slot, xg_out.at[out_half], xg_in, across).start()

    def payload_view(first, count):
        return payload.at[pl.ds(2 * first, 2 * count)]

    payloads = Gather(place, wires, payload_view)
    reduces[0].to_major()
    wires.arrived(payload_slot, payload.at[2 * place.shard + 1 - latent], place.column())
    payloads.minor()
    reduces[2].to_gather()
    reduces[1].to_col()
    payloads.major()
    reduces[0].to_minor()
    reduces[1].to_gather()
    reduces[2].gather.major()
    payloads.cores()
    reduces[0].to_col()
    reduces[1].gather.major()
    reduces[2].gather.cores()
    reduces[0].to_gather()
    payloads.finish()
    payload_copy = pltpu.make_async_copy(payload, payload_hbm, local_sems.at[3])
    payload_copy.start()
    reduces[1].gather.cores()
    reduces[2].gather.finish()
    outs = [
        pltpu.make_async_copy(final.at[seg], final_hbm.at[seg], local_sems.at[4 + seg])
        for seg in range(3)
    ]
    outs[2].start()
    reduces[0].gather.major()
    reduces[1].gather.finish()
    outs[1].start()

    @pl.when(mine)
    def _():
        result_ref[...] = res_out[out_half]
        xgrad_ref[...] = xg_out[out_half]

    @pl.when(jnp.logical_not(mine))
    def _():
        wires.copy(res_slot, res_out.at[out_half], res_in, across).wait_send()
        wires.copy(res_slot, res_out.at[out_half], res_in, back_from).wait_recv()
        wires.copy(xg_slot, xg_out.at[out_half], xg_in, across).wait_send()
        wires.copy(xg_slot, xg_out.at[out_half], xg_in, back_from).wait_recv()
        result_ref[...] = res_in[...]
        xgrad_ref[...] = xg_in[...]

    reduces[0].gather.cores()
    reduces[0].gather.finish()
    outs[0].start()
    x_sent()
    cot_sent()
    wires.drain()
    payload_copy.wait()
    for out in outs:
        out.wait()


def spread_halves(place, wires, source, landing):
    r, c, k, latent = place.r, place.c, place.k, place.latent
    slots = [wires.slot() for _ in range(2)]

    def copy(row, half):
        return pltpu.make_async_remote_copy(
            src_ref=source,
            dst_ref=landing.at[half],
            send_sem=wires.send_sems.at[slots[row]],
            recv_sem=wires.recv_sems.at[slots[half]],
            device_id=place.at(row=jnp.int32(row), col=xor(r, k * row)),
            device_id_type=MESH,
        )

    def each_target(act):
        for row in range(2):
            away = jnp.logical_or(r != row, c != xor(r, k * row))
            for half in range(2):
                @pl.when(jnp.logical_and(away, c == half))
                def _():
                    act(copy(row, half))

    each_target(lambda made: made.start())

    @pl.when(r == latent)
    def _():
        landing[c] = source[...]

    def collect():
        for half in range(2):
            @pl.when(jnp.logical_or(r != latent, c != half))
            def _():
                copy(0, half).wait_recv()

    def sent():
        each_target(lambda made: made.wait_send())

    return slots, collect, sent


def whole(shape, dtype):
    return pltpu.VMEM(shape, dtype)


def run_block(n, x, cot, modp, weights, triple_bias, widening):
    shards = 2 * n * n
    rows = SEG // shards
    tokens = (2, SEQ, HALF)
    vmem = pl.BlockSpec(memory_space=pltpu.VMEM)
    hbm = pl.BlockSpec(memory_space=pl.ANY)
    peers = max(n - 1, 1)
    scratch = [
        whole((3, 2, SEG, HALF), BF16),
        whole(tokens, BF16),
        whole(tokens, BF16),
        whole((4, 8, HALF), F32),
        whole((2, 8, HALF), F32),
        whole(tokens, F32),
        whole((SEQ, 1), F32),
        whole(tokens, BF16),
        whole((3, SEQ, HALF), BF16),
        whole((6, SEQ, SEQ), F32),
        whole((SEQ, HALF), BF16),
        whole(tokens, BF16),
        whole(tokens, BF16),
        whole(tokens, F32),
        whole(tokens, F32),
        whole((SEQ, 1), F32),
        whole(tokens, BF16),
        whole((4, SEQ, HALF), BF16),
        whole((4, SEQ, HALF), F32),
        whole(tokens, BF16),
        whole(tokens, BF16),
        whole(tokens, BF16),
        whole((4, SEQ, HALF), BF16),
        whole(tokens, BF16),
        whole(tokens, BF16),
        whole(tokens, F32),
        whole(tokens, BF16),
        whole((SEQ, HALF), BF16),
        whole((3, SEQ, HALF), BF16),
        whole(tokens, BF16),
        whole(tokens, BF16),
        whole(tokens, BF16),
        whole((SEQ, HALF), BF16),
        whole(tokens, F32),
        whole((SEQ, HALF), F32),
        whole((2, 16, HALF), BF16),
        whole((2 * shards, 16, HALF), BF16),
        whole((3, 2, SEG, HALF), BF16),
        whole((3, 2, SEG // 2, HALF), BF16),
        whole((3, peers, 2, SEG // (2 * n), HALF), BF16),
        whole((3, peers, 2, rows, HALF), BF16),
        whole((3, rows, HALF), BF16),
        whole((3, SEG, HALF), BF16),
        pltpu.SemaphoreType.DMA((SEMS,)),
        pltpu.SemaphoreType.DMA((SEMS,)),
        pltpu.SemaphoreType.DMA((8,)),
    ]

    def body(*refs):
        kernel(n, *refs)

    return pl.pallas_call(
        body,
        out_shape=(
            jax.ShapeDtypeStruct((SEQ, HALF), BF16),
            jax.ShapeDtypeStruct((SEQ, HALF), F32),
            jax.ShapeDtypeStruct((3, SEG, HALF), BF16),
            jax.ShapeDtypeStruct((2 * shards, 16, HALF), BF16),
        ),
        in_specs=[vmem, vmem, vmem, hbm, vmem, vmem],
        out_specs=(vmem, vmem, hbm, hbm),
        scratch_shapes=scratch,
        compiler_params=pltpu.CompilerParams(
            collective_id=0, has_side_effects=True, vmem_limit_bytes=60 * 1024 * 1024
        ),
        name="block",
    )(x, cot, modp, weights, triple_bias, widening)


def body(
    activations,
    timesteps,
    class_labels,
    time_table,
    class_table,
    modulation,
    modulation_bias,
    attention,
    attention_bias,
    projection,
    projection_bias,
    expansion,
    widening_bias,
    reduction,
    narrowing_bias,
    cotangent,
):
    n = math.isqrt(lax.axis_size("dp") // 2)
    latents = 4 * n * n
    dp, row = lax.axis_index("dp"), lax.axis_index("row")
    core, chip = dp % 2, dp // 2
    z, x = chip % n, chip // n
    shard = (core * n + jnp.where(core == 0, x, z)) * n + jnp.where(core == 0, z, x)

    picks = lax.all_gather(
        jnp.stack([timesteps, class_labels], axis=1), ("dp", "col"), axis=0, tiled=True
    ).reshape(n, n, 2, 2, 2)
    picks = jnp.stack([picks[:, :, 0], jnp.swapaxes(picks[:, :, 1], 0, 1)]).reshape(latents, 2)
    time_onehot = (picks[:, 0:1] == jnp.arange(STEPS, dtype=jnp.int32)[None, :]).astype(BF16)
    class_onehot = (picks[:, 1:2] == jnp.arange(CLASSES, dtype=jnp.int32)[None, :]).astype(BF16)
    condition = jnp.dot(time_onehot, time_table, preferred_element_type=F32) + jnp.dot(
        class_onehot, class_table, preferred_element_type=F32
    )
    silu_cond, silu_pullback = jax.vjp(jax.nn.silu, condition)
    silu_low = silu_cond.astype(BF16)
    modulation_flat = modulation.reshape(HALF, 6 * HALF)
    silu_mine = lax.dynamic_slice_in_dim(silu_low, 2 * shard, 2, axis=0)
    parts = jnp.dot(silu_mine, modulation_flat, preferred_element_type=F32).reshape(2, 6, HALF)
    extra = jnp.concatenate(
        [modulation_bias, projection_bias[None], narrowing_bias[None]], axis=0
    ).astype(F32)
    extra = jnp.where(row == 0, extra, 0.0)
    modp = jnp.concatenate([parts, jnp.zeros((2, 2, HALF), F32)], axis=1) + extra[None]

    weights = jnp.stack(
        [
            jnp.concatenate([jnp.swapaxes(attention, 0, 1).reshape(3 * HALF, HALF), projection]),
            jnp.swapaxes(expansion.reshape(HALF, 4, HALF), 0, 1).reshape(SEG, HALF),
            reduction,
        ]
    )
    zero_bias = jnp.zeros_like(attention_bias[0])
    triple_bias = jnp.stack([attention_bias[0], zero_bias, attention_bias[1]])[:, None].astype(F32)
    widening = widening_bias.reshape(4, 1, HALF).astype(F32)
    result, activations_grad, final, payload = run_block(
        n, activations, cotangent, modp, weights, triple_bias, widening
    )

    grad_modulation = payload[:, 0:6].reshape(latents, 6 * HALF)
    modulation_grad = lax.dot_general(
        silu_low, grad_modulation, (((0,), (0,)), ((), ())), preferred_element_type=F32
    )
    small = jnp.sum(payload, axis=0, dtype=F32)
    grad_silu = lax.psum(
        lax.dot_general(
            grad_modulation,
            modulation_flat,
            (((1,), (1,)), ((), ())),
            preferred_element_type=F32,
        ),
        "col",
    )
    grad_condition = silu_pullback(grad_silu)[0]

    def table_product(onehot):
        return lax.dot_general(
            onehot.astype(F32),
            grad_condition,
            (((0,), (0,)), ((), ())),
            precision=lax.Precision.HIGHEST,
        )

    attention_grad = jnp.swapaxes(final[0, : 3 * HALF].reshape(3, HALF, HALF), 0, 1)
    expansion_grad = jnp.swapaxes(final[1].reshape(4, HALF, HALF), 0, 1).reshape(HALF, SEG)
    return (
        result,
        activations_grad,
        table_product(time_onehot),
        table_product(class_onehot),
        modulation_grad.reshape(HALF, 6, HALF),
        small[0:6],
        attention_grad.astype(F32),
        small[8:10],
        final[0, 3 * HALF :].astype(F32),
        small[6],
        expansion_grad.astype(F32),
        small[10:14].reshape(SEG),
        final[2].astype(F32),
        small[7],
    )


def solution(mesh):
    placed = (
        P(("dp", "row"), "col"),
        P(("dp", "col")),
        P(("dp", "col")),
        P(None, "row"),
        P(None, "row"),
        P("row", None, "col"),
        P(None, "col"),
        P("col", None, "row"),
        P(None, "row"),
        P("row", "col"),
        P("col"),
        P("col", "row"),
        P("row"),
        P("row", "col"),
        P("col"),
        P(("dp", "row"), "col"),
    )
    return jax.shard_map(
        body,
        mesh=mesh,
        in_specs=placed,
        out_specs=(
            P(("dp", "row"), "col"),
            P(("dp", "row"), "col"),
            P(None, "row"),
            P(None, "row"),
            P("row", None, "col"),
            P(None, "col"),
            P("col", None, "row"),
            P(None, "row"),
            P("row", "col"),
            P("col"),
            P("col", "row"),
            P("row"),
            P("row", "col"),
            P("col"),
        ),
        check_vma=False,
    )
```

time: 1220 us -> 343 us (0.28)
  waiting for transfers between devices: 888 us -> 12 us
  Pallas kernels: 0 us -> 109 us
  blocking collectives: 211 us -> 168 us
  other arithmetic: 36 us -> 10.3 us
  matrix products: 35.4 us -> 10.1 us
  local copies, waits for them, and re-layouts: 29.8 us -> 17.3 us
    psum x2 -> x1, waiting for transfers between devices: 610 us -> 12 us  [body(): lax.psum(lax.dot_general(grad_modulation, modulation_flat, (((1,), (1,)),...]
    reduce_scatter x8 -> x0, waiting for transfers between devices: 191 us -> none  [the longest x4 140 us: through_rows(): lax.psum_scatter(row_term(jnp.int32(0), keep_rows * lax.axis_size('col'))...]
    psum x5 -> x0, blocking collectives: 153 us -> none  [the longest x1 127 us: body(): lax.psum(modulation_bias_flat.astype(jnp.bfloat16), 'dp')]
    all_gather x7 -> x1, blocking collectives: 49.7 us -> 168 us  [body(): lax.all_gather(jnp.stack([timesteps, class_labels], axis=1), ('dp', 'col'...]
    pallas_call x0 -> x1, Pallas kernels: none -> 109 us  [run_block(): pl.pallas_call(body, out_shape=(jax.ShapeDtypeStruct((SEQ, HALF), BF16),...]
    all_gather x3 -> x0, waiting for transfers between devices: 85.9 us -> none  [through_cols(): gathered = lax.all_gather(local_rows, 'col', axis=0, tiled=True)]
    dot_general x23 -> x7, matrix products: 35.4 us -> 10.1 us  [the longest x2 5.2 us: table_product(): lax.dot_general(onehot.astype(F32), grad_condition, (((0,), (0,)), ((), (...]
    unnamed x137 -> x27, local copies, waits for them, and re-layouts: 24.1 us -> 4.32 us
  transfers between devices with their start and end apart: 13 -> 1, of which waited for: 12 -> 1; matrix products, arithmetic and copies ran while one was open for 4% -> 4% of each run, Pallas kernels for 0% -> 0%
where the time goes in v1:
time: 343 us; the launch traced here: 342 us
  blocking collectives  168 us (49%)
  Pallas kernels  109 us (32%)
  local copies, waits for them, and re-layouts  17.3 us (5%)
  between operations  15.6 us (5%)
  waiting for transfers between devices  12 us (3%)
  other arithmetic  10.3 us (3%)
  matrix products  10.1 us (3%)
    all_gather x1, blocking collectives, body(): lax.all_gather(jnp.stack([timesteps, class_labels], axis=1), ('dp', 'col'...  168 us
    pallas_call x1, Pallas kernels, run_block(): pl.pallas_call(body, out_shape=(jax.ShapeDtypeStruct((SEQ, HALF), BF16),...  109 us
    psum x1, waiting for transfers between devices, body(): lax.psum(lax.dot_general(grad_modulation, modulation_flat, (((1,), (1,)),...  12 us
  transfers between devices with their start and end apart: 1, of which 1 were waited for; matrix products, arithmetic and copies ran while one was open for 4% of the time, Pallas kernels for 0%

profile of v1, /device:TPU:0, one launch (start us, length us, event | category | flops | bytes accessed | tf_op | source)
XLA Modules:
  0.0 342.4 jit_solution(7631941522143185558)
XLA Ops:
  7.2 0.0 copy-start
  7.2 0.0 all-reduce.3.cloned.1.call-start
  8.6 0.7 concatenate.25
  9.3 0.7 concatenate.26
  10.0 0.8 slice_bitcast_fusion.1
  10.8 1.3 reshape.148.refs_5_
  12.1 0.1 add_bitcast_fusion
  12.1 167.6 %all-gather = s32[64,1,2]{2,1,0:T(1,128)S(1)} all-gather(s32[1,1,2]{2,1,0:T(1,128)S(1)} %add_bitcast_fusion), channel_id=1, replica_groups=mesh['dp'=32,'row'=2,'col'=2] {'dp','col'}, dimensions={0}, use_global_device_ids=true | all-gather | bytes 520 | tf_op jit(solution)/shard_map/all_gather | solution.py:882
  179.7 0.1 copy.51
  179.9 0.1 copy.62
  180.0 0.2 copy.54
  180.2 0.1 reshape.142
  180.3 2.4 copy.81
  182.7 2.8 copy.55
  185.6 0.0 copy-start.5
  185.6 0.0 copy-start.9
  185.6 0.3 fusion.8
  185.9 0.3 multiply_convert_fusion
  186.3 0.0 copy-start.11
  186.3 0.0 copy-start.2
  186.3 0.0 copy-start.4
  186.3 0.6 fusion
  186.9 0.1 pad.2.clone
  187.0 0.1 maximum_bitcast_fusion
  187.1 0.6 pad_add_fusion.refs_2_
  187.7 0.7 maximum_convert_fusion.refs_4_
  188.4 2.0 pad_maximum_fusion.refs_3_
  190.4 109.5 %block.1 = (bf16[256,384]{1,0:T(8,128)(2,1)}, f32[256,384]{1,0:T(8,128)}, bf16[3,1536,384]{2,1,0:T(8,128)(2,1)}, bf16[64,16,384]{2,1,0:T(8,128)(2,1)}) custom-call(bf16[256,384]{1,0:T(8,128)(2,1)} %refs_0_.1, bf16[256,384]{1,0:T(8,128)(2,1)} %refs_1_.1, f32[2,8,384]{2,1,0:T(8,128)} %pad_add_fusion.refs_2_, bf16[3,1536,384]{2,1,0:T(8,128)(2,1)} %pad_maximum_fusion.refs_3_, ...), custom_call_target="tpu_custom_call" | custom-call | tf_op jit(solution)/shard_map/block/pallas_call | solution.py:839
  299.9 1.1 slice.54
  301.1 1.3 convolution_bitcast_fusion
  302.4 0.0 all-reduce.3.cloned.1.call-update
  302.4 0.1 convert_reduce_fusion
  302.6 0.6 slice.67
  303.2 0.6 slice.66
  303.8 1.8 bitcast_convert_fusion.1
  305.6 1.3 slice.56
  306.8 3.3 bitcast_convert_fusion
  310.1 0.6 reshape.147
  310.7 1.3 convert_bitcast_fusion.1
  312.0 0.2 convert_bitcast_fusion
  312.2 1.7 copy.69
  313.9 2.4 fusion.2
  316.4 0.6 slice_reduce_fusion
  317.0 12.0 %all-reduce.3.cloned.1.call-done = f32[64,384]{1,0:T(8,128)} async-done(((f32[64,384]{1,0:T(8,128)}), f32[64,384]{1,0:T(8,128)}) %all-reduce.3.cloned.1.call-update) | async-done | bytes 98320 | tf_op jit(solution)/shard_map/psum | solution.py:921
  328.9 3.2 fusion.7
  332.1 2.0 fusion.6
  334.2 0.7 copy.87
  334.8 0.7 copy.88
  (24 shorter events, 0.1 us)
Async XLA Ops:
  7.2 178.8 %copy-start = (bf16[1001,384]{1,0:T(8,128)(2,1)S(1)}, bf16[1001,384]{1,0:T(8,128)(2,1)}, u32[]{:S(2)}) copy-start(bf16[1001,384]{1,0:T(8,128)(2,1)} %param.20) | copy-start | bytes 2306308
  7.2 321.8 %all-reduce.3.cloned.1.call-start = ((), (), s32[]{:S(2)}) async-start(), calls=%async_computation | async-start | bytes 196608 | tf_op jit(solution)/shard_map/psum | solution.py:921
  182.7 2.9 copy-start.6
  185.6 1.4 copy-start.5
  185.6 1.3 copy-start.9
  186.3 0.8 copy-start.11
  186.3 2.1 copy-start.2
  186.3 2.1 copy-start.4
  190.4 110.6 %copy-start.1 = (bf16[384,6,384]{2,0,1:T(8,128)(2,1)S(1)}, bf16[384,6,384]{2,0,1:T(8,128)(2,1)}, u32[]{:S(2)}) copy-start(bf16[384,6,384]{2,0,1:T(8,128)(2,1)} %param.21) | copy-start | bytes 5308420
  299.9 2.5 copy-start.3
  316.4 17.8 %copy-start.10 = (bf16[256,384]{1,0:T(8,128)(2,1)S(1)}, bf16[256,384]{1,0:T(8,128)(2,1)}, u32[]{:S(2)}) copy-start(bf16[256,384]{1,0:T(8,128)(2,1)} %get-tuple-element.48) | copy-start | bytes 589828
  328.9 3.2 copy-start.7
  328.9 5.9 %copy-start.8 = (f32[256,384]{1,0:T(8,128)S(1)}, f32[256,384]{1,0:T(8,128)}, u32[]{:S(2)}) copy-start(f32[256,384]{1,0:T(8,128)} %get-tuple-element.49) | copy-start | bytes 1179652
Sparse Core Ops, SparseCore 0:
  302.5 26.3 all-reduce.2

commit v2 on v1

v2 whole, which is shorter than its diff:
```python
import math

import jax
import jax.numpy as jnp
from jax import lax
from jax.experimental import pallas as pl
from jax.experimental.pallas import tpu as pltpu
from jax.sharding import PartitionSpec as P

D = 768
HALF = 384
SEQ = 256
HEAD_DIM = 64
STEPS = 1000
CLASSES = 1001
SEG = 1536
EPSILON = 1e-06
ROWS = 32
PART = SEQ // 2
SEMS = 176
F32 = jnp.float32
BF16 = jnp.bfloat16
MESH = pl.DeviceIdType.MESH


def dot(u, v):
    return lax.dot_general(u, v, (((1,), (0,)), ((), ())), preferred_element_type=F32)


def dot_nt(u, v):
    return lax.dot_general(u, v, (((1,), (1,)), ((), ())), preferred_element_type=F32)


def dot_tn(u, v):
    return lax.dot_general(u, v, (((0,), (0,)), ((), ())), preferred_element_type=F32)


def xor(u, v):
    return u + v - 2 * u * v


class Place:
    def __init__(self, n):
        self.n = n
        self.dp = lax.axis_index("dp")
        self.r = lax.axis_index("row")
        self.c = lax.axis_index("col")
        self.k = lax.rem(self.dp, 2)
        chip = lax.div(self.dp, 2)
        z = lax.rem(chip, n)
        x = lax.div(chip, n)
        self.major = x * (1 - self.k) + z * self.k
        self.minor = z * (1 - self.k) + x * self.k
        self.shard = (self.k * n + self.major) * n + self.minor
        self.latent = xor(self.c, self.k * self.r)

    def at(self, dp=None, row=None, col=None):
        return {
            "dp": self.dp if dp is None else dp,
            "row": self.r if row is None else row,
            "col": self.c if col is None else col,
        }

    def plane(self, major, minor):
        x = major * (1 - self.k) + minor * self.k
        z = minor * (1 - self.k) + major * self.k
        return self.at(dp=(x * self.n + z) * 2 + self.k)

    def along_minor(self, step):
        return self.plane(self.major, lax.rem(self.minor + step, self.n))

    def along_major(self, step):
        return self.plane(lax.rem(self.major + step, self.n), self.minor)

    def sibling(self):
        return self.at(dp=self.dp + 1 - 2 * self.k)

    def group(self, step):
        row = xor(self.r, step & 1)
        col = xor(self.c, step >> 1)
        return self.at(row=row, col=col)

    def partner(self):
        return self.at(row=1 - self.r, col=xor(self.c, self.k))

    def column(self):
        return self.at(col=1 - self.c)


class Wires:
    def __init__(self, send_sems, recv_sems):
        self.send_sems, self.recv_sems = send_sems, recv_sems
        self.used = 0
        self.sent = []

    def slot(self):
        self.used += 1
        assert self.used <= SEMS
        return self.used - 1

    def copy(self, slot, src, dst, device):
        return pltpu.make_async_remote_copy(
            src_ref=src,
            dst_ref=dst,
            send_sem=self.send_sems.at[slot],
            recv_sem=self.recv_sems.at[slot],
            device_id=device,
            device_id_type=MESH,
        )

    def send(self, slot, src, dst, device):
        copy = self.copy(slot, src, dst, device)
        copy.start()
        self.sent.append(copy)

    def arrived(self, slot, dst, device):
        self.copy(slot, dst, dst, device).wait_recv()

    def drain(self):
        for copy in self.sent:
            copy.wait_send()


class Gather:
    def __init__(self, place, wires, view):
        self.place, self.wires, self.view = place, wires, view
        self.near = [wires.slot() for _ in range(place.n - 1)]
        self.ring = [wires.slot() for _ in range(4)]
        self.core = [wires.slot() for _ in range(4)]

    def base(self, step, core=None):
        p = self.place
        own = core is None
        k, major = (p.k, p.major) if own else (core, p.minor)
        return (k * p.n + lax.rem(major + step, p.n)) * p.n

    def to_sibling(self, step):
        n = self.place.n
        mine = self.view(self.base(step), n)
        self.wires.send(self.core[step], mine, mine, self.place.sibling())

    def minor(self):
        p, w, n = self.place, self.wires, self.place.n
        mine = self.view(p.shard, 1)
        for step in range(1, n):
            w.send(self.near[step - 1], mine, mine, p.along_minor(step))

    def major(self):
        p, w, n = self.place, self.wires, self.place.n
        row = self.base(0)
        for step in range(1, n):
            other = lax.rem(p.minor + n - step, n)
            w.arrived(self.near[step - 1], self.view(row + other, 1), p.along_minor(step))
        if n > 1:
            mine = self.view(row, n)
            w.send(self.ring[0], mine, mine, p.along_major(1))
            w.send(self.ring[1], mine, mine, p.along_major(3))
        self.to_sibling(0)

    def major_on(self):
        p, w, n = self.place, self.wires, self.place.n
        if n == 1:
            return
        before, after = self.base(3), self.base(1)
        w.arrived(self.ring[0], self.view(before, n), p.along_major(3))
        half = self.view(before, 2)
        w.send(self.ring[2], half, half, p.along_major(1))
        w.arrived(self.ring[1], self.view(after, n), p.along_major(1))
        half = self.view(after + 2, 2)
        w.send(self.ring[3], half, half, p.along_major(3))
        self.to_sibling(3)
        self.to_sibling(1)

    def cores(self):
        p, w, n = self.place, self.wires, self.place.n
        if n == 1:
            return
        far = self.base(2)
        w.arrived(self.ring[2], self.view(far, 2), p.along_major(3))
        w.arrived(self.ring[3], self.view(far + 2, 2), p.along_major(1))
        self.to_sibling(2)

    def finish(self):
        p, w, n = self.place, self.wires, self.place.n
        for step in range(n):
            w.arrived(self.core[step], self.view(self.base(step, 1 - p.k), n), p.sibling())


class Reduce:
    def __init__(self, place, wires, seg, grads, from_core, from_major, from_minor, final):
        self.place, self.wires, self.seg = place, wires, seg
        self.grads, self.final = grads, final
        self.from_core, self.from_major = from_core, from_major
        self.from_minor = from_minor
        n = place.n
        self.rows = SEG // (2 * n * n)
        self.core = [wires.slot() for _ in range(n)]
        self.ring = [wires.slot() for _ in range(6)]
        self.near = [wires.slot() for _ in range(2 * n)]
        self.gather = Gather(place, wires, self.final_view)

    def span(self, first, count):
        return pl.ds(pl.multiple_of(first * self.rows, 16), count * self.rows)

    def view(self, first, count):
        return self.grads.at[self.seg, :, self.span(first, count)]

    def final_view(self, first, count):
        return self.final.at[self.seg, self.span(first, count)]

    def base(self, step):
        p = self.place
        return (p.k * p.n + lax.rem(p.major + step, p.n)) * p.n

    def add(self, first, count, arrivals):
        kind = BF16 if len(arrivals) == 1 else F32
        size = count * self.rows
        base, chunk = first * self.rows, 96

        def step(i, carry):
            at = pl.ds(pl.multiple_of(base + i * chunk, 16), chunk)
            total = self.grads[self.seg, :, at].astype(kind)
            for ref, start in arrivals:
                here = pl.ds(pl.multiple_of(start * self.rows + i * chunk, 16), chunk)
                total = total + ref[:, here].astype(kind)
            self.grads[self.seg, :, at] = total.astype(BF16)
            return carry

        lax.fori_loop(0, size // chunk, step, 0)

    def to_core(self):
        p, n = self.place, self.place.n
        for step in (2, 1, 3, 0) if n > 1 else (0,):
            block = lax.rem(p.minor + step, n)
            self.wires.send(
                self.core[step],
                self.view(((1 - p.k) * n + block) * n, n),
                self.from_core.at[self.seg, :, self.span(block * n, n)],
                p.sibling(),
            )

    def add_core(self, step):
        p, n = self.place, self.place.n
        block = lax.rem(p.major + step, n)
        landed = self.from_core.at[self.seg, :, self.span(block * n, n)]
        self.wires.arrived(self.core[step], landed, p.sibling())
        self.add(self.base(step), n, [(self.from_core.at[self.seg], block * n)])

    def ring_send(self, piece, first, step):
        self.wires.send(
            self.ring[piece],
            self.view(first, 2),
            self.from_major.at[self.seg, piece],
            self.place.along_major(step),
        )

    def ring_arrived(self, piece, step):
        self.wires.arrived(
            self.ring[piece], self.from_major.at[self.seg, piece], self.place.along_major(step)
        )
        return (self.from_major.at[self.seg, piece], 0)

    def to_major(self):
        if self.place.n == 1:
            self.add_core(0)
            return
        far, after, before = self.base(2), self.base(1), self.base(3)
        self.add_core(2)
        self.ring_send(0, far, 1)
        self.ring_send(1, far + 2, 3)
        self.add_core(1)
        self.ring_send(3, after + 2, 1)
        self.add_core(3)
        self.ring_send(4, before, 3)

    def major_on(self):
        if self.place.n == 1:
            return
        after, before = self.base(1), self.base(3)
        self.add(after, 2, [self.ring_arrived(0, 3)])
        self.ring_send(2, after, 1)
        self.add(before + 2, 2, [self.ring_arrived(1, 1)])
        self.ring_send(5, before + 2, 3)
        self.add_core(0)

    def to_minor(self):
        p, w, n = self.place, self.wires, self.place.n
        row = self.base(0)
        if n > 1:
            second = [self.ring_arrived(3, 3)]
            first = [self.ring_arrived(4, 1)]
            first.append(self.ring_arrived(2, 3))
            self.add(row, 2, first)
            second.append(self.ring_arrived(5, 1))
            self.add(row + 2, 2, second)
        for side in (1, 0):
            half = 1 - p.c if side else p.c
            for step in range(1 - side, n):
                there = p.along_minor(step)
                there["col"] = half
                w.send(
                    self.near[side * n + step],
                    self.grads.at[
                        self.seg, half, self.span(row + lax.rem(p.minor + step, n), 1)
                    ],
                    self.from_minor.at[self.seg, side * n + step],
                    there,
                )

    def to_gather(self):
        p, w, n = self.place, self.wires, self.place.n
        total = self.grads[self.seg, p.c, self.span(p.shard, 1)].astype(F32)
        for side in (0, 1):
            for step in range(1 - side, n):
                landed = self.from_minor.at[self.seg, side * n + step]
                w.arrived(self.near[side * n + step], landed, p.along_minor(step))
                total = total + landed[...].astype(F32)
        self.final[self.seg, self.span(p.shard, 1)] = total.astype(BF16)
        self.gather.minor()


def kernel(
    n,
    x_ref,
    cot_ref,
    step_ref,
    label_ref,
    time_hbm,
    class_hbm,
    modulation_hbm,
    attention_hbm,
    projection_hbm,
    expansion_hbm,
    reduction_hbm,
    modulation_bias_ref,
    projection_bias_ref,
    narrowing_ref,
    attention_bias_ref,
    widening_ref,
    result_ref,
    xgrad_ref,
    final_hbm,
    rows_ref,
    silu_ref,
    condition_grad_ref,
    weights,
    tables_time,
    tables_class,
    modulation,
    ids_out,
    ids_in,
    modp,
    spread_rows,
    silu_out,
    silu_in,
    x_all,
    cot_all,
    mod_parts,
    mod,
    normed1,
    rstd1,
    hidden1,
    triple,
    probs,
    attended,
    send1,
    recv1,
    branch1,
    normed2,
    rstd2,
    hidden2,
    activated,
    slope,
    grad_b2,
    send2,
    recv2,
    grad_up,
    send3,
    recv3,
    grad_res,
    grad_b1,
    grad_att,
    grad_tri,
    send4,
    recv4,
    res_out,
    res_in,
    xg_out,
    xg_low,
    xg_in,
    payload_out,
    payload,
    grads,
    from_core,
    from_major,
    from_minor,
    final,
    send_sems,
    recv_sems,
    local_sems,
):
    place = Place(n)
    wires = Wires(send_sems, recv_sems)
    r, c, k, latent = place.r, place.c, place.k, place.latent

    own = [
        [
            pltpu.make_async_copy(
                attention_hbm.at[kind],
                weights.at[0, c, kind * HALF : (kind + 1) * HALF],
                local_sems.at[kind],
            )
            for kind in range(3)
        ]
        + [
            pltpu.make_async_copy(
                projection_hbm, weights.at[0, c, 3 * HALF : 4 * HALF], local_sems.at[3]
            )
        ],
        [
            pltpu.make_async_copy(
                expansion_hbm.at[:, block * HALF : (block + 1) * HALF],
                weights.at[1, c, block * HALF : (block + 1) * HALF],
                local_sems.at[4 + block],
            )
            for block in range(4)
        ],
        [pltpu.make_async_copy(reduction_hbm, weights.at[2, c], local_sems.at[8])],
    ]
    table_loads = [
        pltpu.make_async_copy(time_hbm, tables_time, local_sems.at[9]),
        pltpu.make_async_copy(class_hbm, tables_class, local_sems.at[10]),
    ]
    modulation_load = pltpu.make_async_copy(modulation_hbm, modulation, local_sems.at[11])
    for copy in own[0] + table_loads + [modulation_load] + own[1] + own[2]:
        copy.start()
    row_at = lax.broadcasted_iota(jnp.int32, (8, 128), 0)
    ids_out[...] = jnp.where(row_at == 0, step_ref[0], label_ref[0])

    barrier = pltpu.get_barrier_semaphore()
    others = [place.group(s) for s in (1, 2, 3)] + [place.sibling()]
    for step in range(1, n):
        others += [place.along_minor(step), place.along_major(step)]
        there = place.along_minor(step)
        there["col"] = 1 - c
        others.append(there)
    for other in others:
        pl.semaphore_signal(barrier, inc=1, device_id=other, device_id_type=MESH)
    pl.semaphore_wait(barrier, len(others))

    shard_rows = SEG // (2 * n * n)

    def weight_view(seg):
        def view(first, count):
            start = pl.multiple_of(first * shard_rows, 16)
            return weights.at[seg, 1 - c, pl.ds(start, count * shard_rows)]

        return view

    gathers = [Gather(place, wires, weight_view(seg)) for seg in range(3)]
    weight_slots = [wires.slot() for _ in range(3)]
    my_rows = pl.ds(pl.multiple_of(place.shard * shard_rows, 16), shard_rows)

    def weights_out(seg):
        for copy in own[seg]:
            copy.wait()
        mine = weights.at[seg, c, my_rows]
        wires.send(weight_slots[seg], mine, mine, place.column())

    def weights_minor(seg):
        wires.arrived(weight_slots[seg], weights.at[seg, 1 - c, my_rows], place.column())
        gathers[seg].minor()

    weights_out(0)
    ids_slot = wires.slot()
    wires.send(ids_slot, ids_out, ids_in, place.column())
    x_spread = Spread(place, wires, x_ref, x_all)
    weights_out(1)
    weights_out(2)

    def table_rows(steps, labels, count):
        lanes = lax.broadcasted_iota(jnp.int32, (count, STEPS), 1)
        class_lanes = lax.broadcasted_iota(jnp.int32, (count, CLASSES), 1)
        return dot((lanes == steps).astype(BF16), tables_time[...]) + dot(
            (class_lanes == labels).astype(BF16), tables_class[...]
        )

    weights_minor(0)
    wires.arrived(ids_slot, ids_in, place.column())
    x_spread.forward()
    latent_at = lax.broadcasted_iota(jnp.int32, (16, 1), 0)

    def by_latent(row):
        return jnp.where(
            latent_at == c,
            ids_out[row : row + 1, 0:1],
            jnp.where(latent_at == 1 - c, ids_in[row : row + 1, 0:1], -1),
        )

    for copy in table_loads:
        copy.wait()
    modulation_load.wait()
    group_condition = table_rows(by_latent(0), by_latent(1), 16)
    group_silu = (group_condition / (1.0 + jnp.exp(-group_condition))).astype(BF16)
    first_row = (r == 0).astype(F32)
    modulation_bias = modulation_bias_ref[...].astype(F32)
    for kind in range(6):
        part = dot(group_silu, modulation[kind])
        for lat in range(2):
            modp[lat, kind : kind + 1, :] = (
                part[lat : lat + 1, :] + first_row * modulation_bias[kind : kind + 1, :]
            )
    for lat in range(2):
        modp[lat, 6:7, :] = first_row * projection_bias_ref[...].astype(F32).reshape(1, HALF)
        modp[lat, 7:8, :] = first_row * narrowing_ref[...].astype(F32).reshape(1, HALF)
    mod_slots = [wires.slot() for _ in range(3)]
    for step in (1, 2, 3):
        there = place.group(step)
        its_latent = xor(there["col"], k * there["row"])
        wires.send(mod_slots[step - 1], modp.at[its_latent], mod_parts.at[step], there)

    gathers[0].major()
    for step in (1, 2, 3):
        wires.arrived(mod_slots[step - 1], mod_parts.at[step], place.group(step))
    mod[c] = modp[latent] + mod_parts[1]
    mod[1 - c] = mod_parts[2] + mod_parts[3]

    def vec(half, row):
        return mod[half, row : row + 1, :]

    def over_rows(body, init=0, part=None):
        def step(i, carry):
            return body(pl.ds(pl.multiple_of(i * ROWS, ROWS), ROWS), carry)

        steps = SEQ // ROWS
        first, last = (0, steps) if part is None else (part * steps // 2, (part + 1) * steps // 2)
        return lax.fori_loop(first, last, step, init)

    def part_rows(part):
        return pl.ds(part * PART, PART)

    def norm(values):
        average = (
            jnp.sum(values[0], axis=-1, keepdims=True) + jnp.sum(values[1], axis=-1, keepdims=True)
        ) * (1.0 / D)
        square = (
            jnp.sum(values[0] * values[0], axis=-1, keepdims=True)
            + jnp.sum(values[1] * values[1], axis=-1, keepdims=True)
        ) * (1.0 / D)
        inverse = lax.rsqrt(square - average * average + EPSILON)
        return [(v - average) * inverse for v in values], inverse

    def norm_back(grad, normed, inverse):
        average = (
            jnp.sum(grad[0], axis=-1, keepdims=True) + jnp.sum(grad[1], axis=-1, keepdims=True)
        ) * (1.0 / D)
        crossed = (
            jnp.sum(grad[0] * normed[0], axis=-1, keepdims=True)
            + jnp.sum(grad[1] * normed[1], axis=-1, keepdims=True)
        ) * (1.0 / D)
        return [inverse * (g - average - m * crossed) for g, m in zip(grad, normed)]

    def token_sum(v):
        return jnp.sum(v, axis=0, keepdims=True)

    gathers[0].major_on()
    x_spread.collect()
    cot_spread = Spread(place, wires, cot_ref, cot_all)

    def first_norm(rows, carry):
        normed, inverse = norm([x_all[h, rows].astype(F32) for h in range(2)])
        rstd1[rows] = inverse
        for h in range(2):
            normed1[h, rows] = normed[h]
            hidden1[h, rows] = (normed[h] * (1.0 + vec(h, 1)) + vec(h, 0)).astype(BF16)
        return carry

    weights_minor(1)
    over_rows(first_norm)
    gathers[0].cores()
    weights_minor(2)

    def weight(seg, half, block):
        return weights[seg, half, block * HALF : (block + 1) * HALF, :]

    for kind in range(3):
        slope[kind] = dot(hidden1[c], weight(0, c, kind))
    cot_spread.forward()
    gathers[1].major()
    gathers[0].finish()
    gathers[2].major()
    for kind in range(3):
        value = slope[kind] + dot(hidden1[1 - c], weight(0, 1 - c, kind))
        if kind != 1:
            value = value + attention_bias_ref[kind // 2 : kind // 2 + 1, :].astype(F32)
        triple[kind] = value.astype(BF16)
    gathers[1].major_on()

    low_lanes = lax.broadcasted_iota(jnp.int32, (SEQ, 128), 1) < HEAD_DIM

    def one_head(v, head):
        mask = low_lanes if head == 0 else jnp.logical_not(low_lanes)
        return jnp.where(mask, v, jnp.zeros_like(v))

    score_scale = HEAD_DIM ** (-0.5)

    def attend(pair):
        lanes = pl.ds(pair * 128, 128)
        query = triple[0, :, lanes] * BF16(score_scale)
        keys = triple[1, :, lanes]
        values = triple[2, :, lanes]
        mixed = []
        for head in range(2):
            scores = dot_nt(one_head(query, head), keys)
            exponent = jnp.exp(scores - jnp.max(scores, axis=-1, keepdims=True))
            total = jnp.sum(exponent, axis=-1, keepdims=True)
            weights_now = exponent * (1.0 / total)
            probs[2 * pair + head] = weights_now
            mixed.append(dot(weights_now.astype(BF16), values))
        attended[:, lanes] = jnp.where(low_lanes, mixed[0], mixed[1]).astype(BF16)

    attend(0)
    gathers[2].major_on()
    attend(1)
    gathers[1].cores()
    attend(2)
    gathers[2].cores()

    def exchange(part, out, landing, slots):
        rows = part_rows(part)
        wires.send(slots[part], out.at[:, rows], landing.at[:, rows], place.partner())

    def exchanged(part, landing, slots):
        wires.arrived(slots[part], landing.at[:, part_rows(part)], place.partner())

    slots1, slots2, slots3, slots4 = ([wires.slot() for _ in range(2)] for _ in range(4))
    for part in range(2):
        rows = part_rows(part)
        for half in range(2):
            send1[half, rows] = dot(attended[rows, :], weight(0, half, 3)).astype(BF16)
        exchange(part, send1, recv1, slots1)
    cot_spread.collect()
    zero = jnp.zeros((1, HALF), F32)

    def start_back(rows, carry):
        out = []
        for h in range(2):
            low = (cot_all[h, rows].astype(F32) * vec(h, 5)).astype(BF16)
            grad_b2[h, rows] = low
            out.append(carry[h] + token_sum(low.astype(F32)))
        return tuple(out)

    narrowing_sum = over_rows(start_back, (zero, zero))

    def second_norm(rows, carry):
        middle = []
        for h in range(2):
            branch = send1[h, rows].astype(F32) + recv1[h, rows].astype(F32) + vec(h, 6)
            branch1[h, rows] = branch
            middle.append(x_all[h, rows].astype(F32) + vec(h, 2) * branch)
        normed, inverse = norm(middle)
        rstd2[rows] = inverse
        for h in range(2):
            normed2[h, rows] = normed[h]
            hidden2[h, rows] = (normed[h] * (1.0 + vec(h, 4)) + vec(h, 3)).astype(BF16)
        return carry

    root = math.sqrt(2.0 / math.pi)
    widening_sum = [zero] * 4
    for part in range(2):
        rows = part_rows(part)
        exchanged(part, recv1, slots1)
        over_rows(second_norm, part=part)
        if part == 0:
            gathers[1].finish()
        for block in range(4):
            upper = dot(hidden2[0, rows], weight(1, 0, block)) + dot(
                hidden2[1, rows], weight(1, 1, block)
            )
            bias = widening_ref[block * HALF : (block + 1) * HALF].astype(F32)
            upper = upper + bias.reshape(1, HALF)
            squared = upper * upper
            bent = jnp.tanh(root * upper * (1.0 + 0.044715 * squared))
            half_up = 0.5 * (1.0 + bent)
            activated[block, rows] = (upper * half_up).astype(BF16)
            slope[block, rows] = half_up + (0.5 * root) * upper * (1.0 - bent * bent) * (
                1.0 + (3.0 * 0.044715) * squared
            )
        if part == 0:
            gathers[2].finish()
        for block in range(4):
            back = dot_nt(grad_b2[0, rows], weight(2, 0, block)) + dot_nt(
                grad_b2[1, rows], weight(2, 1, block)
            )
            low = (back * slope[block, rows]).astype(BF16)
            grad_up[block, rows] = low
            widening_sum[block] = widening_sum[block] + token_sum(low.astype(F32))
        for half in range(2):
            value = dot_nt(grad_up[0, rows], weight(1, half, 0))
            for block in range(1, 4):
                value = value + dot_nt(grad_up[block, rows], weight(1, half, block))
            send3[half, rows] = value.astype(BF16)
        exchange(part, send3, recv3, slots3)

    reduces = [
        Reduce(place, wires, seg, grads, from_core, from_major, from_minor, final)
        for seg in range(3)
    ]

    def keep_grad(seg, half, block, value):
        grads[seg, half, block * HALF : (block + 1) * HALF, :] = value.astype(BF16)

    for block in range(4):
        for half in range(2):
            keep_grad(2, half, block, dot_tn(activated[block], grad_b2[half]))
    reduces[2].to_core()
    for block in range(4):
        for half in range(2):
            keep_grad(1, half, block, dot_tn(hidden2[half], grad_up[block]))
    reduces[1].to_core()
    for part in range(2):
        rows = part_rows(part)
        for half in range(2):
            value = dot(activated[0, rows], weight(2, half, 0))
            for block in range(1, 4):
                value = value + dot(activated[block, rows], weight(2, half, block))
            send2[half, rows] = value.astype(BF16)
        exchange(part, send2, recv2, slots2)
    reduces[2].to_major()

    def second_back(rows, carry):
        shift, scale, gate, bias = (list(part) for part in carry)
        inverse = rstd2[rows]
        normed = [normed2[h, rows] for h in range(2)]
        scaled = []
        for h in range(2):
            grad = send3[h, rows].astype(F32) + recv3[h, rows].astype(F32)
            shift[h] = shift[h] + token_sum(grad)
            scale[h] = scale[h] + token_sum(grad * normed[h])
            scaled.append(grad * (1.0 + vec(h, 4)))
        back = norm_back(scaled, normed, inverse)
        for h in range(2):
            total = cot_all[h, rows].astype(F32) + back[h]
            grad_res[h, rows] = total
            gate[h] = gate[h] + token_sum(total * branch1[h, rows])
            low = (total * vec(h, 2)).astype(BF16)
            grad_b1[h, rows] = low
            bias[h] = bias[h] + token_sum(low.astype(F32))
        return tuple(shift), tuple(scale), tuple(gate), tuple(bias)

    pair_zero = (zero, zero)
    sums2 = (pair_zero,) * 4
    for part in range(2):
        rows = part_rows(part)
        exchanged(part, recv3, slots3)
        sums2 = over_rows(second_back, sums2, part)
        grad_att[rows, :] = (
            dot_nt(grad_b1[0, rows], weight(0, 0, 3)) + dot_nt(grad_b1[1, rows], weight(0, 1, 3))
        ).astype(BF16)
    shift2, scale2, gate1, projection_sum = sums2
    for half in range(2):
        keep_grad(0, half, 3, dot_tn(attended[...], grad_b1[half]))

    def attend_back(pair):
        lanes = pl.ds(pair * 128, 128)
        query = triple[0, :, lanes] * BF16(score_scale)
        keys = triple[1, :, lanes]
        values = triple[2, :, lanes]
        above = grad_att[:, lanes]
        by_query, by_keys, by_values = [], [], []
        for head in range(2):
            weights_now = probs[2 * pair + head]
            grad_probs = dot_nt(one_head(above, head), values)
            by_values.append(dot_tn(weights_now.astype(BF16), above))
            crossed = jnp.sum(grad_probs * weights_now, axis=-1, keepdims=True)
            low = (weights_now * (grad_probs - crossed)).astype(BF16)
            by_query.append(dot(low, keys) * score_scale)
            by_keys.append(dot_tn(low, query))
        for kind, parts in enumerate((by_query, by_keys, by_values)):
            grad_tri[kind, :, lanes] = jnp.where(low_lanes, parts[0], parts[1]).astype(BF16)

    reduces[2].major_on()
    attend_back(0)
    reduces[1].to_major()
    exchanged(0, recv2, slots2)
    exchanged(1, recv2, slots2)
    mine = r == latent
    self_col = xor(latent, k * latent)
    out_half = c * (r == latent).astype(jnp.int32) + (1 - self_col) * (r != latent).astype(jnp.int32)
    across = place.at(row=latent, col=1 - self_col)
    back_from = place.at(row=1 - r, col=xor(r, k * (1 - r)))

    def branch_end(rows, carry):
        gate = list(carry)
        for h in range(2):
            branch = send2[h, rows].astype(F32) + recv2[h, rows].astype(F32) + vec(h, 7)
            gate[h] = gate[h] + token_sum(cot_all[h, rows].astype(F32) * branch)
            middle = x_all[h, rows].astype(F32) + vec(h, 2) * branch1[h, rows]
            res_out[h, rows] = (middle + vec(h, 5) * branch).astype(BF16)
        return tuple(gate)

    gate2 = over_rows(branch_end, pair_zero)
    res_slot, xg_slot = wires.slot(), wires.slot()

    @pl.when(jnp.logical_not(mine))
    def _():
        wires.copy(res_slot, res_out.at[out_half], res_in, across).start()

    attend_back(1)
    reduces[2].to_minor()
    attend_back(2)
    reduces[1].major_on()
    for half in range(2):
        for kind in range(3):
            keep_grad(0, half, kind, dot_tn(hidden1[half], grad_tri[kind]))
    reduces[0].to_core()
    for part in range(2):
        rows = part_rows(part)
        for half in range(2):
            value = dot_nt(grad_tri[0, rows], weight(0, half, 0))
            for kind in range(1, 3):
                value = value + dot_nt(grad_tri[kind, rows], weight(0, half, kind))
            send4[half, rows] = value.astype(BF16)
        exchange(part, send4, recv4, slots4)
    reduces[2].to_gather()
    reduces[1].to_minor()
    reduces[0].to_major()
    reduces[2].gather.major()

    def first_back(rows, carry):
        shift, scale = (list(part) for part in carry)
        inverse = rstd1[rows]
        normed = [normed1[h, rows] for h in range(2)]
        scaled = []
        for h in range(2):
            grad = send4[h, rows].astype(F32) + recv4[h, rows].astype(F32)
            shift[h] = shift[h] + token_sum(grad)
            scale[h] = scale[h] + token_sum(grad * normed[h])
            scaled.append(grad * (1.0 + vec(h, 1)))
        back = norm_back(scaled, normed, inverse)
        for h in range(2):
            total = grad_res[h, rows] + back[h]
            xg_out[h, rows] = total
            xg_low[h, rows] = total.astype(BF16)
        return tuple(shift), tuple(scale)

    sums1 = (pair_zero,) * 2
    for part in range(2):
        exchanged(part, recv4, slots4)
        sums1 = over_rows(first_back, sums1, part)
    shift1, scale1 = sums1

    def sums(kind):
        return token_sum(grad_tri[kind].astype(F32))

    shared = [sums(0), sums(2)] + widening_sum
    digit = lax.broadcasted_iota(jnp.int32, (1, HALF), 1) < 128
    for row in range(2):
        picked = jnp.where(latent == c, ids_out[row : row + 1, 0:1], ids_in[row : row + 1, 0:1])
        high = lax.shift_right_logical(picked, 5)
        shared.append(jnp.where(digit, high, picked - 32 * high).astype(F32))
    for h in range(2):
        own_rows = [shift1[h], scale1[h], gate1[h], shift2[h], scale2[h], gate2[h]]
        own_rows += [projection_sum[h], narrowing_sum[h]]
        payload_out[h] = jnp.concatenate(own_rows + shared, axis=0).astype(BF16)
    payload_slot = wires.slot()
    spot = 2 * place.shard + latent
    wires.send(payload_slot, payload_out.at[1 - c], payload.at[spot], place.column())
    payload[spot] = payload_out[c]

    @pl.when(jnp.logical_not(mine))
    def _():
        wires.copy(xg_slot, xg_low.at[out_half], xg_in, across).start()

    def payload_view(first, count):
        return payload.at[pl.ds(2 * first, 2 * count)]

    payloads = Gather(place, wires, payload_view)
    reduces[0].major_on()
    wires.arrived(payload_slot, payload.at[2 * place.shard + 1 - latent], place.column())
    payloads.minor()
    reduces[1].to_gather()
    reduces[2].gather.major_on()
    payloads.major()
    reduces[0].to_minor()
    payloads.major_on()
    reduces[1].gather.major()
    reduces[2].gather.cores()
    payloads.cores()
    reduces[1].gather.major_on()
    reduces[0].to_gather()
    payloads.finish()

    count = 4 * n * n
    for lat in range(count):
        for part in range(3):
            spread_rows[part, pl.ds(16 * lat, 16), :] = payload[
                lat, :, part * 128 : (part + 1) * 128
            ].astype(F32)
    for kind in range(16):
        for part in range(3):
            rows_ref[kind, :, part * 128 : (part + 1) * 128] = spread_rows[
                part, pl.ds(kind, count, stride=16), :
            ].astype(BF16)
    reduces[0].gather.major()
    reduces[1].gather.cores()
    value = dot_nt(rows_ref[0], modulation[0])
    for kind in range(1, 6):
        value = value + dot_nt(rows_ref[kind], modulation[kind])
    silu_out[...] = value
    silu_slot = wires.slot()
    wires.send(silu_slot, silu_out, silu_in, place.column())

    reduces[0].gather.major_on()
    reduces[2].gather.finish()
    outs = [
        pltpu.make_async_copy(final.at[seg], final_hbm.at[seg], local_sems.at[12 + seg])
        for seg in range(3)
    ]
    outs[2].start()

    def decode(kind):
        both = rows_ref[kind].astype(F32)
        return (32.0 * both[:, 0:1] + both[:, 128:129]).astype(jnp.int32)

    condition = table_rows(decode(14), decode(15), count)
    sigmoid = 1.0 / (1.0 + jnp.exp(-condition))
    silu_ref[...] = (condition * sigmoid).astype(BF16)
    reduces[0].gather.cores()
    reduces[1].gather.finish()
    outs[1].start()
    wires.arrived(silu_slot, silu_in, place.column())
    condition_grad_ref[...] = (silu_out[...] + silu_in[...]) * (
        sigmoid * (1.0 + condition * (1.0 - sigmoid))
    )

    @pl.when(mine)
    def _():
        result_ref[...] = res_out[out_half]
        xgrad_ref[...] = xg_out[out_half]

    @pl.when(jnp.logical_not(mine))
    def _():
        wires.copy(res_slot, res_out.at[out_half], res_in, across).wait_send()
        wires.copy(res_slot, res_out.at[out_half], res_in, back_from).wait_recv()
        wires.copy(xg_slot, xg_low.at[out_half], xg_in, across).wait_send()
        wires.copy(xg_slot, xg_low.at[out_half], xg_in, back_from).wait_recv()
        result_ref[...] = res_in[...]
        xgrad_ref[...] = xg_in[...].astype(F32)

    reduces[0].gather.finish()
    outs[0].start()
    x_spread.sent()
    cot_spread.sent()
    wires.drain()
    for out in outs:
        out.wait()


class Spread:
    def __init__(self, place, wires, source, landing):
        self.place, self.wires, self.landing = place, wires, landing
        r, c, k, latent = place.r, place.c, place.k, place.latent
        self.mine = r == latent
        self.far = 1 - xor(latent, k * latent)
        self.first, _, self.last = [wires.slot() for _ in range(3)]
        self.out = self.copy(
            source, c, self.first, self.first + c, place.at(row=1 - r, col=xor(r, k * (1 - r)))
        )
        self.forwarded = self.copy(
            landing.at[self.far], self.far, self.last, self.last, place.partner()
        )
        self.out.start()

        @pl.when(self.mine)
        def _():
            landing[c] = source[...]

    def copy(self, source, half, send_slot, recv_slot, there):
        return pltpu.make_async_remote_copy(
            src_ref=source,
            dst_ref=self.landing.at[half],
            send_sem=self.wires.send_sems.at[send_slot],
            recv_sem=self.wires.recv_sems.at[recv_slot],
            device_id=there,
            device_id_type=MESH,
        )

    def arrived(self, half, slot):
        self.copy(self.landing.at[half], half, self.last, slot, self.place.partner()).wait_recv()

    def forward(self):
        @pl.when(jnp.logical_not(self.mine))
        def _():
            self.arrived(self.far, self.first + self.far)
            self.forwarded.start()

    def collect(self):
        @pl.when(self.mine)
        def _():
            self.arrived(self.far, self.last)

        @pl.when(jnp.logical_not(self.mine))
        def _():
            self.arrived(1 - self.far, self.first + 1 - self.far)

    def sent(self):
        self.out.wait_send()

        @pl.when(jnp.logical_not(self.mine))
        def _():
            self.forwarded.wait_send()


def whole(shape, dtype):
    return pltpu.VMEM(shape, dtype)


def run_block(n, *operands):
    shards = 2 * n * n
    rows = SEG // shards
    tokens = (2, SEQ, HALF)
    vmem = pl.BlockSpec(memory_space=pltpu.VMEM)
    hbm = pl.BlockSpec(memory_space=pl.ANY)
    smem = pl.BlockSpec(memory_space=pltpu.SMEM)
    scratch = [
        whole((3, 2, SEG, HALF), BF16),
        whole((STEPS, HALF), BF16),
        whole((CLASSES, HALF), BF16),
        whole((6, HALF, HALF), BF16),
        whole((8, 128), jnp.int32),
        whole((8, 128), jnp.int32),
        whole((2, 8, HALF), F32),
        whole((3, 32 * shards, 128), F32),
        whole((2 * shards, HALF), F32),
        whole((2 * shards, HALF), F32),
        whole(tokens, BF16),
        whole(tokens, BF16),
        whole((4, 8, HALF), F32),
        whole((2, 8, HALF), F32),
        whole(tokens, F32),
        whole((SEQ, 1), F32),
        whole(tokens, BF16),
        whole((3, SEQ, HALF), BF16),
        whole((6, SEQ, SEQ), F32),
        whole((SEQ, HALF), BF16),
        whole(tokens, BF16),
        whole(tokens, BF16),
        whole(tokens, F32),
        whole(tokens, F32),
        whole((SEQ, 1), F32),
        whole(tokens, BF16),
        whole((4, SEQ, HALF), BF16),
        whole((4, SEQ, HALF), F32),
        whole(tokens, BF16),
        whole(tokens, BF16),
        whole(tokens, BF16),
        whole((4, SEQ, HALF), BF16),
        whole(tokens, BF16),
        whole(tokens, BF16),
        whole(tokens, F32),
        whole(tokens, BF16),
        whole((SEQ, HALF), BF16),
        whole((3, SEQ, HALF), BF16),
        whole(tokens, BF16),
        whole(tokens, BF16),
        whole(tokens, BF16),
        whole((SEQ, HALF), BF16),
        whole(tokens, F32),
        whole(tokens, BF16),
        whole((SEQ, HALF), BF16),
        whole((2, 16, HALF), BF16),
        whole((2 * shards, 16, HALF), BF16),
        whole((3, 2, SEG, HALF), BF16),
        whole((3, 2, SEG // 2, HALF), BF16),
        whole((3, 6, 2, 2 * rows, HALF), BF16),
        whole((3, 2 * n, rows, HALF), BF16),
        whole((3, SEG, HALF), BF16),
        pltpu.SemaphoreType.DMA((SEMS,)),
        pltpu.SemaphoreType.DMA((SEMS,)),
        pltpu.SemaphoreType.DMA((16,)),
    ]

    def body(*refs):
        kernel(n, *refs)

    return pl.pallas_call(
        body,
        out_shape=(
            jax.ShapeDtypeStruct((SEQ, HALF), BF16),
            jax.ShapeDtypeStruct((SEQ, HALF), F32),
            jax.ShapeDtypeStruct((3, SEG, HALF), BF16),
            jax.ShapeDtypeStruct((16, 2 * shards, HALF), BF16),
            jax.ShapeDtypeStruct((2 * shards, HALF), BF16),
            jax.ShapeDtypeStruct((2 * shards, HALF), F32),
        ),
        in_specs=[vmem, vmem, smem, smem] + [hbm] * 7 + [vmem] * 5,
        out_specs=(vmem, vmem, hbm, vmem, vmem, vmem),
        scratch_shapes=scratch,
        compiler_params=pltpu.CompilerParams(
            collective_id=0, has_side_effects=True, vmem_limit_bytes=60 * 1024 * 1024
        ),
        name="block",
    )(*operands)


def finish_kernel(
    result_in,
    xgrad_in,
    final_hbm,
    rows_ref,
    silu_ref,
    condition_grad_ref,
    result_ref,
    xgrad_ref,
    time_hbm,
    class_hbm,
    modulation_hbm,
    modulation_bias_ref,
    attention_hbm,
    attention_bias_ref,
    projection_hbm,
    projection_bias_ref,
    expansion_hbm,
    widening_ref,
    reduction_hbm,
    narrowing_ref,
    final,
    time_grad,
    class_grad,
    modulation_grad,
    wide,
    sems,
):
    loads = [pltpu.make_async_copy(final_hbm.at[seg], final.at[seg], sems.at[seg]) for seg in range(3)]
    for seg in (2, 1, 0):
        loads[seg].start()
    stores = []

    def store(source, target):
        copy = pltpu.make_async_copy(source, target, sems.at[3 + len(stores)])
        copy.start()
        stores.append(copy)

    result_ref[...] = result_in[...]
    xgrad_ref[...] = xgrad_in[...]
    silu = silu_ref[...]
    for kind in range(6):
        modulation_grad[kind] = dot_tn(silu, rows_ref[kind])
        store(modulation_grad.at[kind], modulation_hbm.at[kind])

    def widen(seg, block):
        at = pl.ds(block * HALF, HALF)
        wide[seg, at] = final[seg, at].astype(F32)
        return wide.at[seg, at]

    loads[2].wait()
    for block in range(4):
        store(widen(2, block), reduction_hbm.at[pl.ds(block * HALF, HALF)])
    loads[1].wait()
    for block in range(4):
        store(widen(1, block), expansion_hbm.at[:, pl.ds(block * HALF, HALF)])
    loads[0].wait()
    for block in range(3):
        store(widen(0, block), attention_hbm.at[block])
    store(widen(0, 3), projection_hbm)

    count = silu.shape[0]
    grad = condition_grad_ref[...]
    high = grad.astype(BF16)
    rest = grad - high.astype(F32)
    middle = rest.astype(BF16)
    low = (rest - middle.astype(F32)).astype(BF16)

    def scatter(kind, size):
        both = rows_ref[kind].astype(F32)
        picked = (32.0 * both[:, 0:1] + both[:, 128:129]).astype(jnp.int32)
        onehot = (lax.broadcasted_iota(jnp.int32, (count, 1024), 1) == picked).astype(BF16)
        return (dot_tn(onehot, high) + dot_tn(onehot, middle) + dot_tn(onehot, low))[:size]

    time_grad[...] = scatter(14, STEPS)
    store(time_grad, time_hbm)
    class_grad[...] = scatter(15, CLASSES)
    store(class_grad, class_hbm)

    def total(kind):
        return jnp.sum(rows_ref[kind].astype(F32), axis=0, keepdims=True)

    for kind in range(6):
        modulation_bias_ref[kind : kind + 1, :] = total(kind)
    projection_bias_ref[...] = total(6).reshape(HALF)
    narrowing_ref[...] = total(7).reshape(HALF)
    for kind in range(2):
        attention_bias_ref[kind : kind + 1, :] = total(8 + kind)
    for block in range(4):
        widening_ref[block * HALF : (block + 1) * HALF] = total(10 + block).reshape(HALF)
    for copy in stores:
        copy.wait()


def finish(result, xgrad, final, rows, silu, condition_grad):
    vmem = pl.BlockSpec(memory_space=pltpu.VMEM)
    hbm = pl.BlockSpec(memory_space=pl.ANY)
    shapes = [
        ((SEQ, HALF), vmem),
        ((SEQ, HALF), vmem),
        ((STEPS, HALF), hbm),
        ((CLASSES, HALF), hbm),
        ((6, HALF, HALF), hbm),
        ((6, HALF), vmem),
        ((3, HALF, HALF), hbm),
        ((2, HALF), vmem),
        ((HALF, HALF), hbm),
        ((HALF,), vmem),
        ((HALF, SEG), hbm),
        ((SEG,), vmem),
        ((SEG, HALF), hbm),
        ((HALF,), vmem),
    ]
    return pl.pallas_call(
        finish_kernel,
        out_shape=tuple(
            jax.ShapeDtypeStruct(shape, BF16 if i == 0 else F32)
            for i, (shape, _) in enumerate(shapes)
        ),
        in_specs=[vmem, vmem, hbm, vmem, vmem, vmem],
        out_specs=tuple(spec for _, spec in shapes),
        scratch_shapes=[
            whole((3, SEG, HALF), BF16),
            whole((STEPS, HALF), F32),
            whole((CLASSES, HALF), F32),
            whole((6, HALF, HALF), F32),
            whole((3, SEG, HALF), F32),
            pltpu.SemaphoreType.DMA((24,)),
        ],
        compiler_params=pltpu.CompilerParams(vmem_limit_bytes=60 * 1024 * 1024),
        name="finish",
    )(result, xgrad, final, rows, silu, condition_grad)


def body(
    activations,
    timesteps,
    class_labels,
    time_table,
    class_table,
    modulation,
    modulation_bias,
    attention,
    attention_bias,
    projection,
    projection_bias,
    expansion,
    widening_bias,
    reduction,
    narrowing_bias,
    cotangent,
):
    n = math.isqrt(lax.axis_size("dp") // 2)
    result, activations_grad, final, rows, silu, condition_grad = run_block(
        n,
        activations,
        cotangent,
        timesteps,
        class_labels,
        time_table,
        class_table,
        jnp.swapaxes(modulation, 0, 1),
        jnp.swapaxes(attention, 0, 1),
        projection,
        expansion,
        reduction,
        modulation_bias,
        projection_bias,
        narrowing_bias,
        attention_bias,
        widening_bias,
    )
    (
        result,
        activations_grad,
        time_grad,
        class_grad,
        modulation_grad,
        modulation_bias_grad,
        attention_grad,
        attention_bias_grad,
        projection_grad,
        projection_bias_grad,
        expansion_grad,
        expansion_bias_grad,
        reduction_grad,
        reduction_bias_grad,
    ) = finish(result, activations_grad, final, rows, silu, condition_grad)
    return (
        result,
        activations_grad,
        time_grad,
        class_grad,
        jnp.swapaxes(modulation_grad, 0, 1),
        modulation_bias_grad,
        jnp.swapaxes(attention_grad, 0, 1),
        attention_bias_grad,
        projection_grad,
        projection_bias_grad,
        expansion_grad,
        expansion_bias_grad,
        reduction_grad,
        reduction_bias_grad,
    )


def solution(mesh):
    placed = (
        P(("dp", "row"), "col"),
        P(("dp", "col")),
        P(("dp", "col")),
        P(None, "row"),
        P(None, "row"),
        P("row", None, "col"),
        P(None, "col"),
        P("col", None, "row"),
        P(None, "row"),
        P("row", "col"),
        P("col"),
        P("col", "row"),
        P("row"),
        P("row", "col"),
        P("col"),
        P(("dp", "row"), "col"),
    )
    return jax.shard_map(
        body,
        mesh=mesh,
        in_specs=placed,
        out_specs=(
            P(("dp", "row"), "col"),
            P(("dp", "row"), "col"),
            P(None, "row"),
            P(None, "row"),
            P("row", None, "col"),
            P(None, "col"),
            P("col", None, "row"),
            P(None, "row"),
            P("row", "col"),
            P("col"),
            P("col", "row"),
            P("row"),
            P("row", "col"),
            P("col"),
        ),
        check_vma=False,
    )
```

time: 343 us -> 127 us (0.37)
  the two profiles are of different devices: /device:TPU:0 before, /device:TPU:3 now
where the time goes in v2:
time: 127 us
  Pallas kernels  125 us (98%)
  between operations  2.11 us (2%)
    pallas_call x1, Pallas kernels, run_block(): pl.pallas_call(body, out_shape=(jax.ShapeDtypeStruct((SEQ, HALF), BF16),...  115 us
    pallas_call x1, Pallas kernels, finish(): pl.pallas_call(finish_kernel, out_shape=tuple((jax.ShapeDtypeStruct(shape...  10.2 us

profile of v2, /device:TPU:3, one launch (start us, length us, event | category | flops | bytes accessed | tf_op | source)
XLA Modules:
  0.0 127.2 jit_solution(9234933062479658859)
XLA Ops:
  1.9 114.9 %block.1 = (bf16[256,384]{1,0:T(8,128)(2,1)}, f32[256,384]{1,0:T(8,128)}, bf16[3,1536,384]{2,1,0:T(8,128)(2,1)}, bf16[16,64,384]{2,1,0:T(8,128)(2,1)}, bf16[64,384]{1,0:T(8,128)(2,1)}, /*index=5*/f32[64,384]{1,0:T(8,128)}) custom-call(bf16[256,384]{1,0:T(8,128)(2,1)} %refs_0_.1, bf16[256,384]{1,0:T(8,128)(2,1)} %refs_1_.1, s32[1]{0:T(128)S(6)} %copy.30.refs_2_, ...), custom_call_target="tpu_custom_call" | custom-call | tf_op jit(solution)/shard_map/block/pallas_call | solution.py:1087
  116.8 10.2 %finish.1 = (bf16[256,384]{1,0:T(8,128)(2,1)}, f32[256,384]{1,0:T(8,128)}, f32[1000,384]{1,0:T(8,128)}, f32[1001,384]{1,0:T(8,128)}, f32[6,384,384]{2,1,0:T(8,12...) custom-call(bf16[256,384]{1,0:T(8,128)(2,1)} %get-tuple-element.34.r, ...), custom_call_target="tpu_custom_call" | custom-call | tf_op jit(solution)/shard_map/finish/pallas_call | solution.py:1220

commit v3 on v2

--- a/solution.py
+++ b/solution.py
@@ -848,6 +848,8 @@
     for part in range(2):
         exchanged(part, recv4, slots4)
         sums1 = over_rows(first_back, sums1, part)
+        if part == 0:
+            reduces[0].major_on()
     shift1, scale1 = sums1
 
     def sums(kind):
@@ -868,27 +870,29 @@
     wires.send(payload_slot, payload_out.at[1 - c], payload.at[spot], place.column())
     payload[spot] = payload_out[c]
 
+    def payload_view(first, count):
+        return payload.at[pl.ds(2 * first, 2 * count)]
+
+    payloads = Gather(place, wires, payload_view)
+    reduces[0].to_minor()
+    wires.arrived(payload_slot, payload.at[2 * place.shard + 1 - latent], place.column())
+    payloads.minor()
+
     @pl.when(jnp.logical_not(mine))
     def _():
         wires.copy(xg_slot, xg_low.at[out_half], xg_in, across).start()
 
-    def payload_view(first, count):
-        return payload.at[pl.ds(2 * first, 2 * count)]
-
-    payloads = Gather(place, wires, payload_view)
-    reduces[0].major_on()
-    wires.arrived(payload_slot, payload.at[2 * place.shard + 1 - latent], place.column())
-    payloads.minor()
     reduces[1].to_gather()
     reduces[2].gather.major_on()
     payloads.major()
-    reduces[0].to_minor()
+    reduces[0].to_gather()
     payloads.major_on()
     reduces[1].gather.major()
     reduces[2].gather.cores()
+    reduces[0].gather.major()
     payloads.cores()
     reduces[1].gather.major_on()
-    reduces[0].to_gather()
+    reduces[0].gather.major_on()
     payloads.finish()
 
     count = 4 * n * n
@@ -902,8 +906,8 @@
             rows_ref[kind, :, part * 128 : (part + 1) * 128] = spread_rows[
                 part, pl.ds(kind, count, stride=16), :
             ].astype(BF16)
-    reduces[0].gather.major()
     reduces[1].gather.cores()
+    reduces[0].gather.cores()
     value = dot_nt(rows_ref[0], modulation[0])
     for kind in range(1, 6):
         value = value + dot_nt(rows_ref[kind], modulation[kind])
@@ -911,7 +915,6 @@
     silu_slot = wires.slot()
     wires.send(silu_slot, silu_out, silu_in, place.column())
 
-    reduces[0].gather.major_on()
     reduces[2].gather.finish()
     outs = [
         pltpu.make_async_copy(final.at[seg], final_hbm.at[seg], local_sems.at[12 + seg])
@@ -926,9 +929,10 @@
     condition = table_rows(decode(14), decode(15), count)
     sigmoid = 1.0 / (1.0 + jnp.exp(-condition))
     silu_ref[...] = (condition * sigmoid).astype(BF16)
-    reduces[0].gather.cores()
     reduces[1].gather.finish()
     outs[1].start()
+    reduces[0].gather.finish()
+    outs[0].start()
     wires.arrived(silu_slot, silu_in, place.column())
     condition_grad_ref[...] = (silu_out[...] + silu_in[...]) * (
         sigmoid * (1.0 + condition * (1.0 - sigmoid))
@@ -948,8 +952,6 @@
         result_ref[...] = res_in[...]
         xgrad_ref[...] = xg_in[...].astype(F32)
 
-    reduces[0].gather.finish()
-    outs[0].start()
     x_spread.sent()
     cot_spread.sent()
     wires.drain()
@@ -1144,9 +1146,9 @@
 
     result_ref[...] = result_in[...]
     xgrad_ref[...] = xgrad_in[...]
-    silu = silu_ref[...]
+    silu = silu_ref[...].T
     for kind in range(6):
-        modulation_grad[kind] = dot_tn(silu, rows_ref[kind])
+        modulation_grad[kind] = dot(silu, rows_ref[kind])
         store(modulation_grad.at[kind], modulation_hbm.at[kind])
 
     def widen(seg, block):
@@ -1165,7 +1167,7 @@
         store(widen(0, block), attention_hbm.at[block])
     store(widen(0, 3), projection_hbm)
 
-    count = silu.shape[0]
+    count = silu_ref.shape[0]
     grad = condition_grad_ref[...]
     high = grad.astype(BF16)
     rest = grad - high.astype(F32)
@@ -1176,7 +1178,8 @@
         both = rows_ref[kind].astype(F32)
         picked = (32.0 * both[:, 0:1] + both[:, 128:129]).astype(jnp.int32)
         onehot = (lax.broadcasted_iota(jnp.int32, (count, 1024), 1) == picked).astype(BF16)
-        return (dot_tn(onehot, high) + dot_tn(onehot, middle) + dot_tn(onehot, low))[:size]
+        onehot = onehot.T
+        return (dot(onehot, high) + dot(onehot, middle) + dot(onehot, low))[:size]
 
     time_grad[...] = scatter(14, STEPS)
     store(time_grad, time_hbm)

time: 127 us -> 127 us (level)
  the two profiles are of different devices: /device:TPU:3 before, /device:TPU:0 now
where the time goes in v3:
time: 127 us
  Pallas kernels  125 us (98%)
  between operations  2.11 us (2%)
    pallas_call x1, Pallas kernels, run_block(): pl.pallas_call(body, out_shape=(jax.ShapeDtypeStruct((SEQ, HALF), BF16),...  114 us
    pallas_call x1, Pallas kernels, finish(): pl.pallas_call(finish_kernel, out_shape=tuple((jax.ShapeDtypeStruct(shape...  10.2 us

profile of v3, /device:TPU:0, one launch (start us, length us, event | category | flops | bytes accessed | tf_op | source)
XLA Modules:
  0.0 126.7 jit_solution(84785672954215306)
XLA Ops:
  1.9 114.3 %block.1 = (bf16[256,384]{1,0:T(8,128)(2,1)}, f32[256,384]{1,0:T(8,128)}, bf16[3,1536,384]{2,1,0:T(8,128)(2,1)}, bf16[16,64,384]{2,1,0:T(8,128)(2,1)}, bf16[64,384]{1,0:T(8,128)(2,1)}, /*index=5*/f32[64,384]{1,0:T(8,128)}) custom-call(bf16[256,384]{1,0:T(8,128)(2,1)} %refs_0_.1, bf16[256,384]{1,0:T(8,128)(2,1)} %refs_1_.1, s32[1]{0:T(128)S(6)} %copy.30.refs_2_, ...), custom_call_target="tpu_custom_call" | custom-call | tf_op jit(solution)/shard_map/block/pallas_call | solution.py:1089
  116.2 10.2 %finish.1 = (bf16[256,384]{1,0:T(8,128)(2,1)}, f32[256,384]{1,0:T(8,128)}, f32[1000,384]{1,0:T(8,128)}, f32[1001,384]{1,0:T(8,128)}, f32[6,384,384]{2,1,0:T(8,12...) custom-call(bf16[256,384]{1,0:T(8,128)(2,1)} %get-tuple-element.34.r, ...), custom_call_target="tpu_custom_call" | custom-call | tf_op jit(solution)/shard_map/finish/pallas_call | solution.py:1223

commit v4 on v3

--- a/solution.py
+++ b/solution.py
@@ -665,6 +665,14 @@
             hidden2[h, rows] = (normed[h] * (1.0 + vec(h, 4)) + vec(h, 3)).astype(BF16)
         return carry
 
+    reduces = [
+        Reduce(place, wires, seg, grads, from_core, from_major, from_minor, final)
+        for seg in range(3)
+    ]
+
+    def keep_grad(seg, half, block, value):
+        grads[seg, half, block * HALF : (block + 1) * HALF, :] = value.astype(BF16)
+
     root = math.sqrt(2.0 / math.pi)
     widening_sum = [zero] * 4
     for part in range(2):
@@ -688,6 +696,11 @@
             )
         if part == 0:
             gathers[2].finish()
+        else:
+            for block in range(4):
+                for half in range(2):
+                    keep_grad(2, half, block, dot_tn(activated[block], grad_b2[half]))
+            reduces[2].to_core()
         for block in range(4):
             back = dot_nt(grad_b2[0, rows], weight(2, 0, block)) + dot_nt(
                 grad_b2[1, rows], weight(2, 1, block)
@@ -702,22 +715,11 @@
             send3[half, rows] = value.astype(BF16)
         exchange(part, send3, recv3, slots3)
 
-    reduces = [
-        Reduce(place, wires, seg, grads, from_core, from_major, from_minor, final)
-        for seg in range(3)
-    ]
-
-    def keep_grad(seg, half, block, value):
-        grads[seg, half, block * HALF : (block + 1) * HALF, :] = value.astype(BF16)
-
-    for block in range(4):
-        for half in range(2):
-            keep_grad(2, half, block, dot_tn(activated[block], grad_b2[half]))
-    reduces[2].to_core()
     for block in range(4):
         for half in range(2):
             keep_grad(1, half, block, dot_tn(hidden2[half], grad_up[block]))
     reduces[1].to_core()
+    reduces[2].to_major()
     for part in range(2):
         rows = part_rows(part)
         for half in range(2):
@@ -726,7 +728,6 @@
                 value = value + dot(activated[block, rows], weight(2, half, block))
             send2[half, rows] = value.astype(BF16)
         exchange(part, send2, recv2, slots2)
-    reduces[2].to_major()
 
     def second_back(rows, carry):
         shift, scale, gate, bias = (list(part) for part in carry)
@@ -1134,9 +1135,20 @@
     wide,
     sems,
 ):
-    loads = [pltpu.make_async_copy(final_hbm.at[seg], final.at[seg], sems.at[seg]) for seg in range(3)]
+    loads = [
+        [
+            pltpu.make_async_copy(
+                final_hbm.at[seg, pl.ds(block * HALF, HALF)],
+                final.at[seg, pl.ds(block * HALF, HALF)],
+                sems.at[24 + 4 * seg + block],
+            )
+            for block in range(4)
+        ]
+        for seg in range(3)
+    ]
     for seg in (2, 1, 0):
-        loads[seg].start()
+        for load in loads[seg]:
+            load.start()
     stores = []
 
     def store(source, target):
@@ -1152,17 +1164,15 @@
         store(modulation_grad.at[kind], modulation_hbm.at[kind])
 
     def widen(seg, block):
+        loads[seg][block].wait()
         at = pl.ds(block * HALF, HALF)
         wide[seg, at] = final[seg, at].astype(F32)
         return wide.at[seg, at]
 
-    loads[2].wait()
     for block in range(4):
         store(widen(2, block), reduction_hbm.at[pl.ds(block * HALF, HALF)])
-    loads[1].wait()
     for block in range(4):
         store(widen(1, block), expansion_hbm.at[:, pl.ds(block * HALF, HALF)])
-    loads[0].wait()
     for block in range(3):
         store(widen(0, block), attention_hbm.at[block])
     store(widen(0, 3), projection_hbm)
@@ -1234,7 +1244,7 @@
             whole((CLASSES, HALF), F32),
             whole((6, HALF, HALF), F32),
             whole((3, SEG, HALF), F32),
-            pltpu.SemaphoreType.DMA((24,)),
+            pltpu.SemaphoreType.DMA((40,)),
         ],
         compiler_params=pltpu.CompilerParams(vmem_limit_bytes=60 * 1024 * 1024),
         name="finish",

time: 127 us -> 125 us (0.984)
  Pallas kernels: 125 us -> 123 us
    pallas_call x1, Pallas kernels: 114 us -> 113 us  [run_block(): pl.pallas_call(body, out_shape=(jax.ShapeDtypeStruct((SEQ, HALF), BF16),...]
where the time goes in v4:
time: 125 us
  Pallas kernels  123 us (98%)
  between operations  2.11 us (2%)
    pallas_call x1, Pallas kernels, run_block(): pl.pallas_call(body, out_shape=(jax.ShapeDtypeStruct((SEQ, HALF), BF16),...  113 us
    pallas_call x1, Pallas kernels, finish(): pl.pallas_call(finish_kernel, out_shape=tuple((jax.ShapeDtypeStruct(shape...  9.77 us

profile of v4, /device:TPU:0, one launch (start us, length us, event | category | flops | bytes accessed | tf_op | source)
XLA Modules:
  0.0 124.6 jit_solution(17266174555763514990)
XLA Ops:
  1.9 112.8 %block.1 = (bf16[256,384]{1,0:T(8,128)(2,1)}, f32[256,384]{1,0:T(8,128)}, bf16[3,1536,384]{2,1,0:T(8,128)(2,1)}, bf16[16,64,384]{2,1,0:T(8,128)(2,1)}, bf16[64,384]{1,0:T(8,128)(2,1)}, /*index=5*/f32[64,384]{1,0:T(8,128)}) custom-call(bf16[256,384]{1,0:T(8,128)(2,1)} %refs_0_.1, bf16[256,384]{1,0:T(8,128)(2,1)} %refs_1_.1, s32[1]{0:T(128)S(6)} %copy.30.refs_2_, ...), custom_call_target="tpu_custom_call" | custom-call | tf_op jit(solution)/shard_map/block/pallas_call | solution.py:1090
  114.7 9.8 %finish.1 = (bf16[256,384]{1,0:T(8,128)(2,1)}, f32[256,384]{1,0:T(8,128)}, f32[1000,384]{1,0:T(8,128)}, f32[1001,384]{1,0:T(8,128)}, f32[6,384,384]{2,1,0:T(8,12...) custom-call(bf16[256,384]{1,0:T(8,128)(2,1)} %get-tuple-element.34.r, ...), custom_call_target="tpu_custom_call" | custom-call | tf_op jit(solution)/shard_map/finish/pallas_call | solution.py:1233

commit v5 on v4

--- a/solution.py
+++ b/solution.py
@@ -520,6 +520,7 @@
         wires.send(mod_slots[step - 1], modp.at[its_latent], mod_parts.at[step], there)
 
     gathers[0].major()
+    weights_minor(1)
     for step in (1, 2, 3):
         wires.arrived(mod_slots[step - 1], mod_parts.at[step], place.group(step))
     mod[c] = modp[latent] + mod_parts[1]
@@ -575,10 +576,9 @@
             hidden1[h, rows] = (normed[h] * (1.0 + vec(h, 1)) + vec(h, 0)).astype(BF16)
         return carry
 
-    weights_minor(1)
+    weights_minor(2)
     over_rows(first_norm)
     gathers[0].cores()
-    weights_minor(2)
 
     def weight(seg, half, block):
         return weights[seg, half, block * HALF : (block + 1) * HALF, :]

time: 125 us -> 124 us (level)
  Pallas kernels: 123 us -> 120 us
    pallas_call x1, Pallas kernels: 113 us -> 111 us  [run_block(): pl.pallas_call(body, out_shape=(jax.ShapeDtypeStruct((SEQ, HALF), BF16),...]
where the time goes in v5:
time: 124 us; the launch traced here: 123 us
  Pallas kernels  120 us (97%)
  between operations  2.11 us (2%)
    pallas_call x1, Pallas kernels, run_block(): pl.pallas_call(body, out_shape=(jax.ShapeDtypeStruct((SEQ, HALF), BF16),...  111 us
    pallas_call x1, Pallas kernels, finish(): pl.pallas_call(finish_kernel, out_shape=tuple((jax.ShapeDtypeStruct(shape...  9.77 us

profile of v5, /device:TPU:0, one launch (start us, length us, event | category | flops | bytes accessed | tf_op | source)
XLA Modules:
  0.0 122.5 jit_solution(15778238607324557555)
XLA Ops:
  1.9 110.7 %block.1 = (bf16[256,384]{1,0:T(8,128)(2,1)}, f32[256,384]{1,0:T(8,128)}, bf16[3,1536,384]{2,1,0:T(8,128)(2,1)}, bf16[16,64,384]{2,1,0:T(8,128)(2,1)}, bf16[64,384]{1,0:T(8,128)(2,1)}, /*index=5*/f32[64,384]{1,0:T(8,128)}) custom-call(bf16[256,384]{1,0:T(8,128)(2,1)} %refs_0_.1, bf16[256,384]{1,0:T(8,128)(2,1)} %refs_1_.1, s32[1]{0:T(128)S(6)} %copy.30.refs_2_, ...), custom_call_target="tpu_custom_call" | custom-call | tf_op jit(solution)/shard_map/block/pallas_call | solution.py:1090
  112.6 9.8 %finish.1 = (bf16[256,384]{1,0:T(8,128)(2,1)}, f32[256,384]{1,0:T(8,128)}, f32[1000,384]{1,0:T(8,128)}, f32[1001,384]{1,0:T(8,128)}, f32[6,384,384]{2,1,0:T(8,12...) custom-call(bf16[256,384]{1,0:T(8,128)(2,1)} %get-tuple-element.34.r, ...), custom_call_target="tpu_custom_call" | custom-call | tf_op jit(solution)/shard_map/finish/pallas_call | solution.py:1233
